TPU v7x, 128 devices: a whole 4x4x4 slice. The times are simulated.
128 devices in a mesh: tok: 4 (over x_lo, core), wid: 8 (over z, x_hi), hid: 4 (over y).
Axes of the slice: x: 4 (x_hi: 2, x_lo: 2; x = x_hi * 2 + x_lo), y: 4, z: 4, core: 2. Of those that a mesh axis runs over, the one named last changes fastest.
Arguments:
- tokens: bfloat16 [1024, 6144], P(('tok', 'hid'), 'wid'), may hold values from -6 to 6
- up_weight: bfloat16 [6144, 24576], P('wid', ('hid', 'tok')), may hold values from -0.109375 to 0.109375
- down_weight: bfloat16 [24576, 6144], P(('hid', 'tok'), 'wid'), may hold values from -0.0546875 to 0.0546875
- cotangent: bfloat16 [1024, 6144], P(('tok', 'hid'), 'wid'), may hold values from -6 to 6
Outputs:
- layer_out: bfloat16 [1024, 6144], P(('tok', 'hid'), 'wid')
- tokens_grad: bfloat16 [1024, 6144], P(('tok', 'hid'), 'wid')
- up_grad: bfloat16 [6144, 24576], P('wid', ('hid', 'tok'))
- down_grad: bfloat16 [24576, 6144], P(('hid', 'tok'), 'wid')
All inputs are finite; a program needn't handle non-finite values.
Results may differ from a plain program's by a relative error of at most 0.025.
Values may be sent and summed in bfloat16 or wider, within the bound.
No kernel may reach another device: no remote copies, remote signals or barrier semaphores. Data moves between devices by JAX's collectives and lax.ppermute only.
A program may use at most 128 MiB of HBM per device.

v0:
```python
import math

import jax
import jax.numpy as jnp
from jax import lax
from jax.sharding import PartitionSpec as P

tanh_scale = math.sqrt(2.0 / math.pi)
cubic_coef = 0.044715


def gelu_parts(preact):
    inner = tanh_scale * (preact + cubic_coef * preact * preact * preact)
    hyper = jnp.tanh(inner)
    activated = 0.5 * preact * (1.0 + hyper)
    derivative = 0.5 * (1.0 + hyper) + 0.5 * preact * (1.0 - hyper * hyper) * tanh_scale * (
        1.0 + 3.0 * cubic_coef * preact * preact
    )
    return (activated, derivative)


def contract_last(left, right):
    return lax.dot_general(
        left, right, (((1,), (1,)), ((), ())), preferred_element_type=jnp.float32
    )


def local(tokens, up_weight, down_weight, cotangent):
    tok_count = lax.axis_size("tok")
    rows_all = lax.all_gather(tokens, "hid", axis=0, tiled=True)
    up_block = lax.all_gather(up_weight, "tok", axis=1, tiled=True)
    down_block = lax.all_gather(down_weight, "tok", axis=0, tiled=True)
    pre_terms = jnp.dot(rows_all, up_block, preferred_element_type=jnp.float32)
    preact = lax.psum_scatter(
        pre_terms.astype(jnp.bfloat16), "wid", scatter_dimension=1, tiled=True
    ).astype(jnp.float32)
    activated, derivative = gelu_parts(preact)
    act_block = lax.all_gather(activated.astype(jnp.bfloat16), "wid", axis=1, tiled=True)
    out_terms = jnp.dot(act_block, down_block, preferred_element_type=jnp.float32)
    layer_out = lax.psum_scatter(
        out_terms.astype(jnp.bfloat16), "hid", scatter_dimension=0, tiled=True
    )
    cot_all = lax.all_gather(cotangent, "hid", axis=0, tiled=True)
    grad_terms = contract_last(cot_all, down_block)
    act_grad = lax.psum_scatter(
        grad_terms.astype(jnp.bfloat16), "wid", scatter_dimension=1, tiled=True
    ).astype(jnp.float32)
    hgrad_block = lax.all_gather(
        (act_grad * derivative).astype(jnp.bfloat16), "wid", axis=1, tiled=True
    )
    back_terms = contract_last(hgrad_block, up_block)
    tokens_grad = lax.psum_scatter(
        back_terms.astype(jnp.bfloat16), "hid", scatter_dimension=0, tiled=True
    )
    grad_scale = 1.0 / math.sqrt(rows_all.shape[0] * tok_count)
    up_terms = jnp.dot(rows_all.T, hgrad_block, preferred_element_type=jnp.float32)
    up_total = lax.psum_scatter(
        up_terms.astype(jnp.bfloat16), "tok", scatter_dimension=1, tiled=True
    ).astype(jnp.float32)
    down_terms = jnp.dot(act_block.T, cot_all, preferred_element_type=jnp.float32)
    down_total = lax.psum_scatter(
        down_terms.astype(jnp.bfloat16), "tok", scatter_dimension=0, tiled=True
    ).astype(jnp.float32)
    up_grad = (up_total * grad_scale).astype(jnp.bfloat16)
    down_grad = (down_total * grad_scale).astype(jnp.bfloat16)
    return (layer_out, tokens_grad, up_grad, down_grad)


def solution(mesh):
    in_specs = (
        P(("tok", "hid"), "wid"),
        P("wid", ("hid", "tok")),
        P(("hid", "tok"), "wid"),
        P(("tok", "hid"), "wid"),
    )
    out_specs = (
        P(("tok", "hid"), "wid"),
        P(("tok", "hid"), "wid"),
        P("wid", ("hid", "tok")),
        P(("hid", "tok"), "wid"),
    )
    return jax.shard_map(local, mesh=mesh, in_specs=in_specs, out_specs=out_specs, check_vma=False)
```

profile of v0, /device:TPU:0, one launch (start us, length us, event | category | flops | bytes accessed | tf_op | source)
XLA Modules:
  0.0 722.3 jit_solution(12510517804511220232)
XLA Ops:
  7.2 0.7 all-gather.9.cloned.1.call-update
  8.0 0.7 all-gather.5.cloned.1.call-update
  8.7 13.1 %all_gather.22 = bf16[256,768]{1,0:T(8,128)(2,1)S(1)} all-gather(bf16[64,768]{1,0:T(8,128)(2,1)S(1)} %copy-done.1), channel_id=1, replica_groups=mesh['tok'=4,'wid'=8,'hid'=4] {'hid'}, dimensions={0}, use_global_device_ids=true | all-gather | bytes 491520 | tf_op jit(solution)/shard_map/all_gather | solution.py:43
  21.8 79.0 %all-gather.9.cloned.1.call-done = bf16[6144,768]{1,0:T(8,128)(2,1)} async-done(((bf16[1536,768]{1,0:T(8,128)(2,1)}), bf16[6144,768]{1,0:T(8,128)(2,1)}) %all-gather.9.cloned.1.call-update) | async-done | bytes 9437200 | tf_op jit(solution)/shard_map/all_gather | solution.py:32
  100.9 11.1 %convolution_convert_fusion.2 = bf16[256,6144]{1,0:T(8,128)(2,1)} fusion(bf16[256,768]{1,0:T(8,128)(2,1)S(1)} %all_gather.22, bf16[6144,768]{1,0:T(8,128)(2,1)} %all-gather.9.cloned.1.call-done), kind=kOutput, calls=%fused_computation.3 | convolution fusion | flops 2417491968 | bytes 12976128 | tf_op jit(solution)/shard_map/dot_general | solution.py:23
  112.0 0.0 reduce-scatter.7.cloned.1.call-start
  112.0 0.8 copy-done.2
  112.9 13.2 %all_gather.18 = bf16[256,768]{1,0:T(8,128)(2,1)S(1)} all-gather(bf16[64,768]{1,0:T(8,128)(2,1)S(1)} %copy-done.2), channel_id=1, replica_groups=mesh['tok'=4,'wid'=8,'hid'=4] {'hid'}, dimensions={0}, use_global_device_ids=true | all-gather | bytes 491520 | tf_op jit(solution)/shard_map/all_gather | solution.py:30
  126.1 67.5 %all-gather.5.cloned.1.call-done = bf16[768,6144]{1,0:T(8,128)(2,1)} async-done(((bf16[768,1536]{1,0:T(8,128)(2,1)}), bf16[768,6144]{1,0:T(8,128)(2,1)}) %all-gather.5.cloned.1.call-update) | async-done | bytes 9437200 | tf_op jit(solution)/shard_map/all_gather | solution.py:31
  193.5 7.7 %convolution_convert_fusion.3 = bf16[256,6144]{1,0:T(8,128)(2,1)} fusion(bf16[256,768]{1,0:T(8,128)(2,1)S(1)} %all_gather.18, bf16[768,6144]{1,0:T(8,128)(2,1)} %all-gather.5.cloned.1.call-done), kind=kOutput, calls=%fused_computation.4 | convolution fusion | flops 2417491968 | bytes 12976128 | tf_op jit(solution)/shard_map/dot_general | solution.py:33
  201.3 0.0 all-gather.11.cloned.1.call-start
  201.3 77.9 %reduce-scatter.11.cloned.1.call-done = bf16[256,768]{1,0:T(8,128)(2,1)} async-done(((bf16[256,6144]{1,0:T(8,128)(2,1)}), bf16[256,768]{1,0:T(8,128)(2,1)}) %reduce-scatter.11.cloned.1.call-update) | async-done | bytes 393232 | tf_op jit(solution)/shard_map/reduce_scatter | solution.py:45
  279.2 82.0 %reduce-scatter.7.cloned.1.call-done = bf16[256,768]{1,0:T(8,128)(2,1)} async-done(((bf16[256,6144]{1,0:T(8,128)(2,1)}), bf16[256,768]{1,0:T(8,128)(2,1)}) %reduce-scatter.7.cloned.1.call-update) | async-done | bytes 393232 | tf_op jit(solution)/shard_map/reduce_scatter | solution.py:34
  361.2 2.6 fusion.8
  363.8 0.0 all-gather.7.cloned.1.call-start
  363.8 0.5 all-gather.7.cloned.1.call-update
  364.4 60.8 %all-gather.11.cloned.1.call-done = bf16[256,6144]{1,0:T(8,128)(2,1)} async-done(((bf16[256,768]{1,0:T(8,128)(2,1)}), bf16[256,6144]{1,0:T(8,128)(2,1)}) %all-gather.11.cloned.1.call-update) | async-done | bytes 3145744 | tf_op jit(solution)/shard_map/all_gather | solution.py:48
  425.3 8.3 %fusion = bf16[768,6144]{0,1:T(8,128)(2,1)} fusion(bf16[256,6144]{1,0:T(8,128)(2,1)} %all-gather.11.cloned.1.call-done, bf16[256,768]{1,0:T(8,128)(2,1)S(1)} %all_gather.18), kind=kOutput, calls=%fused_computation.2 | convolution fusion | flops 2420637696 | bytes 12976128 | tf_op jit(solution)/shard_map/dot_general | solution.py:56
  433.6 0.0 reduce-scatter.17.cloned.1.call-start
  433.6 54.7 %all-gather.7.cloned.1.call-done = bf16[256,6144]{1,0:T(8,128)(2,1)} async-done(((bf16[256,768]{1,0:T(8,128)(2,1)}), bf16[256,6144]{1,0:T(8,128)(2,1)}) %all-gather.7.cloned.1.call-update) | async-done | bytes 3145744 | tf_op jit(solution)/shard_map/all_gather | solution.py:38
  488.3 8.2 %convolution_convert_fusion = bf16[6144,768]{1,0:T(8,128)(2,1)} fusion(bf16[256,6144]{1,0:T(8,128)(2,1)} %all-gather.7.cloned.1.call-done, bf16[256,768]{1,0:T(8,128)(2,1)S(1)} %all_gather.22), kind=kOutput, calls=%fused_computation | convolution fusion | flops 2420637696 | bytes 12976128 | tf_op jit(solution)/shard_map/dot_general | solution.py:60
  496.6 0.2 reduce-scatter.13.cloned.1.call-start
  496.8 8.9 %convolution_convert_fusion.4 = bf16[256,768]{1,0:T(8,128)(2,1)} fusion(bf16[256,6144]{1,0:T(8,128)(2,1)} %all-gather.11.cloned.1.call-done, bf16[768,6144]{1,0:T(8,128)(2,1)} %all-gather.5.cloned.1.call-done), kind=kOutput, calls=%fused_computation.14 | convolution fusion | flops 2416115712 | bytes 12976128 | tf_op jit(solution)/shard_map/dot_general | solution.py:23
  505.7 0.0 reduce-scatter.9.cloned.1.call-start
  505.7 7.1 convolution_convert_fusion.5
  512.9 63.2 %reduce-scatter.15.cloned.1.call-done = bf16[768,1536]{0,1:T(8,128)(2,1)} async-done(((bf16[768,6144]{0,1:T(8,128)(2,1)}), bf16[768,1536]{0,1:T(8,128)(2,1)}) %reduce-scatter.15.cloned.1.call-update) | async-done | bytes 2359312 | tf_op jit(solution)/shard_map/reduce_scatter | solution.py:57
  576.1 2.1 multiply_convert_fusion.1
  578.2 2.4 copy.8
  580.6 86.5 %reduce-scatter.17.cloned.1.call-done = bf16[1536,768]{1,0:T(8,128)(2,1)} async-done(((bf16[6144,768]{1,0:T(8,128)(2,1)}), bf16[1536,768]{1,0:T(8,128)(2,1)}) %reduce-scatter.17.cloned.1.call-update) | async-done | bytes 2359312 | tf_op jit(solution)/shard_map/reduce_scatter | solution.py:61
  667.1 3.5 multiply_convert_fusion
  670.6 21.3 %reduce-scatter.13.cloned.1.call-done = bf16[64,768]{1,0:T(8,128)(2,1)} async-done(((bf16[256,768]{1,0:T(8,128)(2,1)}), bf16[64,768]{1,0:T(8,128)(2,1)}) %reduce-scatter.13.cloned.1.call-update) | async-done | bytes 98320 | tf_op jit(solution)/shard_map/reduce_scatter | solution.py:52
  691.9 23.6 %reduce-scatter.9.cloned.1.call-done = bf16[64,768]{1,0:T(8,128)(2,1)} async-done(((bf16[256,768]{1,0:T(8,128)(2,1)}), bf16[64,768]{1,0:T(8,128)(2,1)}) %reduce-scatter.9.cloned.1.call-update) | async-done | bytes 98320 | tf_op jit(solution)/shard_map/reduce_scatter | solution.py:40
  (16 shorter events, 0.3 us)
Async XLA Ops:
  7.2 1.5 copy-start.1
  7.2 93.7 %all-gather.9.cloned.1.call-start = ((), (), s32[]{:S(2)}) async-start(), calls=%async_computation.9 | async-start | bytes 11796480 | tf_op jit(solution)/shard_map/all_gather | solution.py:32
  7.9 185.6 %all-gather.5.cloned.1.call-start = ((), (), s32[]{:S(2)}) async-start(), calls=%async_computation.6 | async-start | bytes 11796480 | tf_op jit(solution)/shard_map/all_gather | solution.py:31
  8.7 270.5 %reduce-scatter.11.cloned.1.call-start = ((), (), s32[]{:S(2)}) async-start(), calls=%async_computation.11 | async-start | bytes 3538944 | tf_op jit(solution)/shard_map/reduce_scatter | solution.py:45
  112.0 0.9 copy-start.2
  112.0 249.2 %reduce-scatter.7.cloned.1.call-start = ((), (), s32[]{:S(2)}) async-start(), calls=%async_computation.7 | async-start | bytes 3538944 | tf_op jit(solution)/shard_map/reduce_scatter | solution.py:34
  201.3 224.0 %all-gather.11.cloned.1.call-start = ((), (), s32[]{:S(2)}) async-start(), calls=%async_computation.12 | async-start | bytes 3538944 | tf_op jit(solution)/shard_map/all_gather | solution.py:48
  363.8 124.5 %all-gather.7.cloned.1.call-start = ((), (), s32[]{:S(2)}) async-start(), calls=%async_computation.8 | async-start | bytes 3538944 | tf_op jit(solution)/shard_map/all_gather | solution.py:38
  364.4 211.7 %reduce-scatter.15.cloned.1.call-start = ((), (), s32[]{:S(2)}) async-start(), calls=%async_computation.14 | async-start | bytes 11796480 | tf_op jit(solution)/shard_map/reduce_scatter | solution.py:57
  433.6 233.5 %reduce-scatter.17.cloned.1.call-start = ((), (), s32[]{:S(2)}) async-start(), calls=%async_computation.15 | async-start | bytes 11796480 | tf_op jit(solution)/shard_map/reduce_scatter | solution.py:61
  496.5 9.2 %copy-start = (bf16[256,6144]{1,0:T(8,128)(2,1)S(1)}, bf16[256,6144]{1,0:T(8,128)(2,1)}, u32[]{:S(2)}) copy-start(bf16[256,6144]{1,0:T(8,128)(2,1)} %all-gather.7.cloned.1.call-done) | copy-start | bytes 9437188
  496.6 195.3 %reduce-scatter.13.cloned.1.call-start = ((), (), s32[]{:S(2)}) async-start(), calls=%async_computation.13 | async-start | bytes 491520 | tf_op jit(solution)/shard_map/reduce_scatter | solution.py:52
  505.7 209.8 %reduce-scatter.9.cloned.1.call-start = ((), (), s32[]{:S(2)}) async-start(), calls=%async_computation.10 | async-start | bytes 491520 | tf_op jit(solution)/shard_map/reduce_scatter | solution.py:40
Sparse Core Ops, SparseCore 0:
  9.7 91.1 all-gather.8
  102.5 90.9 all-gather.4
  197.4 81.7 reduce-scatter.10
  282.9 78.2 reduce-scatter.6
  363.9 61.2 all-gather.10
  428.0 60.2 all-gather.6
  490.8 85.2 reduce-scatter.14
  578.5 88.5 reduce-scatter.16
  670.0 21.8 reduce-scatter.12
  694.8 20.5 reduce-scatter.8
where the time goes:
time: 723 us; the launch traced here: 722 us
  waiting for transfers between devices  618 us (85%)
  matrix products  51.3 us (7%)
  blocking collectives  26.3 us (4%)
  between operations  14.2 us (2%)
  other arithmetic  8.18 us (1%)
    reduce_scatter x1, waiting for transfers between devices, local(): lax.psum_scatter(down_terms.astype(jnp.bfloat16), 'tok', scatter_dimensio...  86.5 us
    reduce_scatter x1, waiting for transfers between devices, local(): lax.psum_scatter(pre_terms.astype(jnp.bfloat16), 'wid', scatter_dimension...  82 us
    all_gather x1, waiting for transfers between devices, local(): down_block = lax.all_gather(down_weight, 'tok', axis=0, tiled=True)  79 us
    reduce_scatter x1, waiting for transfers between devices, local(): lax.psum_scatter(grad_terms.astype(jnp.bfloat16), 'wid', scatter_dimensio...  77.9 us
    all_gather x1, waiting for transfers between devices, local(): up_block = lax.all_gather(up_weight, 'tok', axis=1, tiled=True)  67.5 us
    reduce_scatter x1, waiting for transfers between devices, local(): lax.psum_scatter(up_terms.astype(jnp.bfloat16), 'tok', scatter_dimension=...  63.2 us
    all_gather x1, waiting for transfers between devices, local(): lax.all_gather((act_grad * derivative).astype(jnp.bfloat16), 'wid', axis=...  60.8 us
    all_gather x1, waiting for transfers between devices, local(): lax.all_gather(activated.astype(jnp.bfloat16), 'wid', axis=1, tiled=True)  54.7 us
  transfers between devices with their start and end apart: 10, of which 10 were waited for; matrix products, arithmetic and copies ran while one was open for 8% of the time, Pallas kernels for 0%

commit v1 on v0

v1 whole, which is shorter than its diff:
```python
import math

import jax
import jax.numpy as jnp
from jax import lax
from jax.sharding import PartitionSpec as P

tanh_scale = math.sqrt(2.0 / math.pi)
cubic_coef = 0.044715


def gelu_parts(preact):
    inner = tanh_scale * (preact + cubic_coef * preact * preact * preact)
    hyper = jnp.tanh(inner)
    activated = 0.5 * preact * (1.0 + hyper)
    derivative = 0.5 * (1.0 + hyper) + 0.5 * preact * (1.0 - hyper * hyper) * tanh_scale * (
        1.0 + 3.0 * cubic_coef * preact * preact
    )
    return (activated, derivative)


def contract(left, right, left_dim, right_dim):
    return lax.dot_general(
        left,
        right,
        (((left_dim,), (right_dim,)), ((), ())),
        preferred_element_type=jnp.float32,
    )


def local(tokens, up_weight, down_weight, cotangent):
    rows = ("tok", "hid")
    tok_all = lax.all_gather(tokens, rows, axis=0, tiled=True)
    cot_all = lax.all_gather(cotangent, rows, axis=0, tiled=True)
    pre_terms = contract(tok_all, up_weight, 1, 0).astype(jnp.bfloat16)
    preact = lax.psum_scatter(pre_terms, "wid", scatter_dimension=0, tiled=True)
    grad_terms = contract(cot_all, down_weight, 1, 1).astype(jnp.bfloat16)
    act_grad = lax.psum_scatter(grad_terms, "wid", scatter_dimension=0, tiled=True)
    activated, derivative = gelu_parts(preact.astype(jnp.float32))
    act_block = lax.all_gather(activated.astype(jnp.bfloat16), "wid", axis=0, tiled=True)
    pre_grad = (act_grad.astype(jnp.float32) * derivative).astype(jnp.bfloat16)
    hgrad_block = lax.all_gather(pre_grad, "wid", axis=0, tiled=True)
    out_terms = contract(act_block, down_weight, 1, 0).astype(jnp.bfloat16)
    layer_out = lax.psum_scatter(out_terms, rows, scatter_dimension=0, tiled=True)
    back_terms = contract(hgrad_block, up_weight, 1, 1).astype(jnp.bfloat16)
    tokens_grad = lax.psum_scatter(back_terms, rows, scatter_dimension=0, tiled=True)
    grad_scale = 1.0 / math.sqrt(tok_all.shape[0])
    down_grad = (contract(act_block, cot_all, 0, 0) * grad_scale).astype(jnp.bfloat16)
    up_grad = (contract(tok_all, hgrad_block, 0, 0) * grad_scale).astype(jnp.bfloat16)
    return (layer_out, tokens_grad, up_grad, down_grad)


def solution(mesh):
    in_specs = (
        P(("tok", "hid"), "wid"),
        P("wid", ("hid", "tok")),
        P(("hid", "tok"), "wid"),
        P(("tok", "hid"), "wid"),
    )
    out_specs = (
        P(("tok", "hid"), "wid"),
        P(("tok", "hid"), "wid"),
        P("wid", ("hid", "tok")),
        P(("hid", "tok"), "wid"),
    )
    return jax.shard_map(local, mesh=mesh, in_specs=in_specs, out_specs=out_specs, check_vma=False)
```

time: 723 us -> 538 us (0.74)
  waiting for transfers between devices: 618 us -> 479 us
  blocking collectives: 26.3 us -> 0 us
  matrix products: 51.3 us -> 36.8 us
    reduce_scatter x6 -> x4, waiting for transfers between devices: 354 us -> 265 us  [the longest x1 81.9 us: local(): preact = lax.psum_scatter(pre_terms, 'wid', scatter_dimension=0, tiled=True)]
    all_gather x4, waiting for transfers between devices: 262 us -> 212 us  [the longest x1 61.1 us: local(): lax.all_gather(activated.astype(jnp.bfloat16), 'wid', axis=0, tiled=True)]
    all_gather x2 -> x0, blocking collectives: 26.3 us -> none  [the longest x1 13.2 us: local(): rows_all = lax.all_gather(tokens, 'hid', axis=0, tiled=True)]
    dot_general x6, matrix products: 51.3 us -> 36.8 us  [contract(): lax.dot_general(left, right, (((left_dim,), (right_dim,)), ((), ())), pre...]
  transfers between devices with their start and end apart: 10 -> 8, of which waited for: 10 -> 8; matrix products, arithmetic and copies ran while one was open for 8% -> 8% of each run, Pallas kernels for 0% -> 0%
where the time goes in v1:
time: 538 us
  waiting for transfers between devices  479 us (89%)
  matrix products  36.8 us (7%)
  between operations  14.1 us (3%)
    reduce_scatter x1, waiting for transfers between devices, local(): preact = lax.psum_scatter(pre_terms, 'wid', scatter_dimension=0, tiled=True)  81.9 us
    reduce_scatter x1, waiting for transfers between devices, local(): lax.psum_scatter(grad_terms, 'wid', scatter_dimension=0, tiled=True)  78.5 us
    reduce_scatter x1, waiting for transfers between devices, local(): lax.psum_scatter(back_terms, rows, scatter_dimension=0, tiled=True)  64.8 us
    all_gather x1, waiting for transfers between devices, local(): lax.all_gather(activated.astype(jnp.bfloat16), 'wid', axis=0, tiled=True)  61.1 us
    all_gather x1, waiting for transfers between devices, local(): hgrad_block = lax.all_gather(pre_grad, 'wid', axis=0, tiled=True)  57.5 us
    all_gather x1, waiting for transfers between devices, local(): cot_all = lax.all_gather(cotangent, rows, axis=0, tiled=True)  49.7 us
    all_gather x1, waiting for transfers between devices, local(): tok_all = lax.all_gather(tokens, rows, axis=0, tiled=True)  44.1 us
    reduce_scatter x1, waiting for transfers between devices, local(): lax.psum_scatter(out_terms, rows, scatter_dimension=0, tiled=True)  39.7 us
  transfers between devices with their start and end apart: 8, of which 8 were waited for; matrix products, arithmetic and copies ran while one was open for 8% of the time, Pallas kernels for 0%

profile of v1, /device:TPU:0, one launch (start us, length us, event | category | flops | bytes accessed | tf_op | source)
XLA Modules:
  0.0 537.5 jit_solution(16028581560602329874)
XLA Ops:
  7.2 0.0 all-gather.9.cloned.1.call-start
  7.2 0.7 all-gather.9.cloned.1.call-update
  7.9 0.0 all-gather.5.cloned.1.call-start
  8.0 0.7 all-gather.5.cloned.1.call-update
  8.7 0.0 reduce-scatter.9.cloned.1.call-start
  8.7 49.7 %all-gather.9.cloned.1.call-done = bf16[1024,768]{1,0:T(8,128)(2,1)} async-done(((bf16[64,768]{1,0:T(8,128)(2,1)}), bf16[1024,768]{1,0:T(8,128)(2,1)}) %all-gather.9.cloned.1.call-update) | async-done | bytes 1572880 | tf_op jit(solution)/shard_map/all_gather | solution.py:34
  58.5 5.5 %convolution_convert_fusion = bf16[1024,1536]{1,0:T(8,128)(2,1)} fusion(bf16[1024,768]{1,0:T(8,128)(2,1)} %all-gather.9.cloned.1.call-done, bf16[1536,768]{1,0:T(8,128)(2,1)S(1)} %copy-done), kind=kOutput, calls=%fused_computation.2 | convolution fusion | flops 2417491968 | bytes 7077888 | tf_op jit(solution)/shard_map/dot_general | solution.py:23
  63.9 0.0 reduce-scatter.9.cloned.1.call-update
  63.9 0.0 reduce-scatter.5.cloned.1.call-start
  64.0 44.1 %all-gather.5.cloned.1.call-done = bf16[1024,768]{1,0:T(8,128)(2,1)} async-done(((bf16[64,768]{1,0:T(8,128)(2,1)}), bf16[1024,768]{1,0:T(8,128)(2,1)}) %all-gather.5.cloned.1.call-update) | async-done | bytes 1572880 | tf_op jit(solution)/shard_map/all_gather | solution.py:33
  108.0 6.4 %convolution_convert_fusion.1 = bf16[1024,1536]{1,0:T(8,128)(2,1)} fusion(bf16[1024,768]{1,0:T(8,128)(2,1)} %all-gather.5.cloned.1.call-done, bf16[768,1536]{1,0:T(8,128)(2,1)} %param.5), kind=kOutput, calls=%fused_computation.3 | convolution fusion | flops 2417491968 | bytes 7077888 | tf_op jit(solution)/shard_map/dot_general | solution.py:23
  114.5 0.0 reduce-scatter.5.cloned.1.call-update
  114.5 0.0 all-gather.7.cloned.1.call-start
  114.5 78.5 %reduce-scatter.9.cloned.1.call-done = bf16[128,1536]{1,0:T(8,128)(2,1)} async-done(((bf16[1024,1536]{1,0:T(8,128)(2,1)}), bf16[128,1536]{1,0:T(8,128)(2,1)}) %reduce-scatter.9.cloned.1.call-update) | async-done | bytes 393232 | tf_op jit(solution)/shard_map/reduce_scatter | solution.py:38
  193.0 81.9 %reduce-scatter.5.cloned.1.call-done = bf16[128,1536]{1,0:T(8,128)(2,1)} async-done(((bf16[1024,1536]{1,0:T(8,128)(2,1)}), bf16[128,1536]{1,0:T(8,128)(2,1)}) %reduce-scatter.5.cloned.1.call-update) | async-done | bytes 393232 | tf_op jit(solution)/shard_map/reduce_scatter | solution.py:36
  274.9 2.6 fusion.8
  277.5 0.0 all-gather.7.cloned.1.call-update
  277.5 0.0 all-gather.11.cloned.1.call-start
  277.6 0.5 all-gather.11.cloned.1.call-update
  278.1 0.0 reduce-scatter.7.cloned.1.call-start
  278.2 61.1 %all-gather.7.cloned.1.call-done = bf16[1024,1536]{1,0:T(8,128)(2,1)} async-done(((bf16[128,1536]{1,0:T(8,128)(2,1)}), bf16[1024,1536]{1,0:T(8,128)(2,1)}) %all-gather.7.cloned.1.call-update) | async-done | bytes 3145744 | tf_op jit(solution)/shard_map/all_gather | solution.py:40
  339.3 5.6 %convolution_convert_fusion.3 = bf16[1024,768]{1,0:T(8,128)(2,1)} fusion(bf16[1024,1536]{1,0:T(8,128)(2,1)} %all-gather.7.cloned.1.call-done, bf16[1536,768]{1,0:T(8,128)(2,1)S(1)} %copy-done), kind=kOutput, calls=%fused_computation.13 | convolution fusion | flops 2416705536 | bytes 7077888 | tf_op jit(solution)/shard_map/dot_general | solution.py:23
  344.9 0.0 reduce-scatter.7.cloned.1.call-update
  344.9 0.2 reduce-scatter.11.cloned.1.call-start
  345.2 57.5 %all-gather.11.cloned.1.call-done = bf16[1024,1536]{1,0:T(8,128)(2,1)} async-done(((bf16[128,1536]{1,0:T(8,128)(2,1)}), bf16[1024,1536]{1,0:T(8,128)(2,1)}) %all-gather.11.cloned.1.call-update) | async-done | bytes 3145744 | tf_op jit(solution)/shard_map/all_gather | solution.py:42
  402.6 6.4 %convolution_convert_fusion.2 = bf16[1024,768]{1,0:T(8,128)(2,1)} fusion(bf16[1024,1536]{1,0:T(8,128)(2,1)} %all-gather.11.cloned.1.call-done, bf16[768,1536]{1,0:T(8,128)(2,1)} %param.5), kind=kOutput, calls=%fused_computation.12 | convolution fusion | flops 2416705536 | bytes 7077888 | tf_op jit(solution)/shard_map/dot_general | solution.py:23
  409.0 0.0 reduce-scatter.11.cloned.1.call-update
  409.1 6.5 %fusion = bf16[768,1536]{0,1:T(8,128)(2,1)} fusion(bf16[1024,1536]{1,0:T(8,128)(2,1)} %all-gather.11.cloned.1.call-done, bf16[1024,768]{1,0:T(8,128)(2,1)} %all-gather.5.cloned.1.call-done), kind=kOutput, calls=%fused_computation.4 | convolution fusion | flops 2418278400 | bytes 7077888 | tf_op jit(solution)/shard_map/dot_general | solution.py:23
  415.5 4.3 copy.8
  419.8 6.4 %multiply_convert_fusion = bf16[1536,768]{1,0:T(8,128)(2,1)} fusion(bf16[1024,1536]{1,0:T(8,128)(2,1)} %all-gather.7.cloned.1.call-done, bf16[1024,768]{1,0:T(8,128)(2,1)} %all-gather.9.cloned.1.call-done), kind=kOutput, calls=%fused_computation | convolution fusion | flops 2418278400 | bytes 7077888 | tf_op jit(solution)/shard_map/dot_general | solution.py:23
  426.2 39.7 %reduce-scatter.7.cloned.1.call-done = bf16[64,768]{1,0:T(8,128)(2,1)} async-done(((bf16[1024,768]{1,0:T(8,128)(2,1)}), bf16[64,768]{1,0:T(8,128)(2,1)}) %reduce-scatter.7.cloned.1.call-update) | async-done | bytes 98320 | tf_op jit(solution)/shard_map/reduce_scatter | solution.py:44
  465.9 64.8 %reduce-scatter.11.cloned.1.call-done = bf16[64,768]{1,0:T(8,128)(2,1)} async-done(((bf16[1024,768]{1,0:T(8,128)(2,1)}), bf16[64,768]{1,0:T(8,128)(2,1)}) %reduce-scatter.11.cloned.1.call-update) | async-done | bytes 98320 | tf_op jit(solution)/shard_map/reduce_scatter | solution.py:46
  (2 shorter events, 0.0 us)
Async XLA Ops:
  7.2 51.3 %copy-start = (bf16[1536,768]{1,0:T(8,128)(2,1)S(1)}, bf16[1536,768]{1,0:T(8,128)(2,1)}, u32[]{:S(2)}) copy-start(bf16[1536,768]{1,0:T(8,128)(2,1)} %param.6) | copy-start | bytes 7077892
  7.2 51.3 %all-gather.9.cloned.1.call-start = ((), (), s32[]{:S(2)}) async-start(), calls=%async_computation.8 | async-start | bytes 1671168 | tf_op jit(solution)/shard_map/all_gather | solution.py:34
  7.9 100.1 %all-gather.5.cloned.1.call-start = ((), (), s32[]{:S(2)}) async-start(), calls=%async_computation.4 | async-start | bytes 1671168 | tf_op jit(solution)/shard_map/all_gather | solution.py:33
  8.7 184.3 %reduce-scatter.9.cloned.1.call-start = ((), (), s32[]{:S(2)}) async-start(), calls=%async_computation.9 | async-start | bytes 3538944 | tf_op jit(solution)/shard_map/reduce_scatter | solution.py:38
  63.9 211.0 %reduce-scatter.5.cloned.1.call-start = ((), (), s32[]{:S(2)}) async-start(), calls=%async_computation.5 | async-start | bytes 3538944 | tf_op jit(solution)/shard_map/reduce_scatter | solution.py:36
  114.5 224.8 %all-gather.7.cloned.1.call-start = ((), (), s32[]{:S(2)}) async-start(), calls=%async_computation.6 | async-start | bytes 3538944 | tf_op jit(solution)/shard_map/all_gather | solution.py:40
  277.5 125.1 %all-gather.11.cloned.1.call-start = ((), (), s32[]{:S(2)}) async-start(), calls=%async_computation.10 | async-start | bytes 3538944 | tf_op jit(solution)/shard_map/all_gather | solution.py:42
  278.1 187.8 %reduce-scatter.7.cloned.1.call-start = ((), (), s32[]{:S(2)}) async-start(), calls=%async_computation.7 | async-start | bytes 1671168 | tf_op jit(solution)/shard_map/reduce_scatter | solution.py:44
  344.9 185.7 %reduce-scatter.11.cloned.1.call-start = ((), (), s32[]{:S(2)}) async-start(), calls=%async_computation.11 | async-start | bytes 1671168 | tf_op jit(solution)/shard_map/reduce_scatter | solution.py:46
Sparse Core Ops, SparseCore 0:
  9.7 48.7 all-gather.8
  60.1 47.8 all-gather.4
  111.9 81.0 reduce-scatter.8
  196.7 78.1 reduce-scatter.4
  277.6 61.5 all-gather.6
  342.0 60.5 all-gather.10
  405.6 60.2 reduce-scatter.6
  469.0 61.6 reduce-scatter.10

commit v2 on v1

v2 whole, which is shorter than its diff:
```python
import math

import jax
import jax.numpy as jnp
from jax import lax
from jax.sharding import Mesh
from jax.sharding import PartitionSpec as P

tanh_scale = math.sqrt(2.0 / math.pi)
cubic_coef = 0.044715
AXES = ("xl", "c", "z", "xh", "y")


def gelu_parts(preact):
    inner = tanh_scale * (preact + cubic_coef * preact * preact * preact)
    hyper = jnp.tanh(inner)
    activated = 0.5 * preact * (1.0 + hyper)
    derivative = 0.5 * (1.0 + hyper) + 0.5 * preact * (1.0 - hyper * hyper) * tanh_scale * (
        1.0 + 3.0 * cubic_coef * preact * preact
    )
    return (activated, derivative)


def contract(left, right, left_dim, right_dim):
    return lax.dot_general(
        left,
        right,
        (((left_dim,), (right_dim,)), ((), ())),
        preferred_element_type=jnp.float32,
    )


def low(value):
    return value.astype(jnp.bfloat16)


def wide(value):
    return value.astype(jnp.float32)


def send(value, axis, step):
    count = lax.axis_size(axis)
    return lax.ppermute(value, axis, [(i, (i + step) % count) for i in range(count)])


def relative(value):
    value = value.reshape(4, 2, 8, value.shape[-1])
    value = lax.dynamic_slice_in_dim(jnp.concatenate([value, value], 0), lax.axis_index("z"), 4, 0)
    return lax.dynamic_slice_in_dim(jnp.concatenate([value, value], 1), lax.axis_index("xh"), 2, 1)


def absolute(value):
    width = value.shape[-1]
    value = lax.dynamic_slice_in_dim(
        jnp.concatenate([value, value], 1), (2 - lax.axis_index("xh")) % 2, 2, 1
    )
    value = lax.dynamic_slice_in_dim(
        jnp.concatenate([value, value], 0), (4 - lax.axis_index("z")) % 4, 4, 0
    )
    return value.reshape(64, width)


def gather_groups(value):
    value = value[:, :, None]
    value = jnp.concatenate([value, send(value, "xl", 1)], 2)
    value = jnp.concatenate([value] + [send(value, "y", -d) for d in (1, 2, 3)], 2)
    return jnp.concatenate([value, send(value, "c", 1)], 2)


def scatter_groups(value):
    value = low(wide(value[:, :, :8]) + wide(send(value[:, :, 8:], "c", 1)))
    total = wide(value[:, :, :2])
    for d in (1, 2, 3):
        total = total + wide(send(value[:, :, 2 * d : 2 * d + 2], "y", d))
    value = low(total)
    return wide(value[:, :, 0]) + wide(send(value[:, :, 1], "xl", 1))


def scatter_wid(blocks):
    up_one = send(blocks[2][0], "z", 1)
    down_one = send(blocks[2][1], "z", -1)
    to_next = jnp.stack([low(wide(blocks[1][0]) + wide(up_one)), blocks[1][1]])
    to_last = jnp.stack([blocks[3][0], low(wide(blocks[3][1]) + wide(down_one))])
    total = wide(blocks[0]) + wide(send(to_next, "z", 1)) + wide(send(to_last, "z", -1))
    return total[0] + wide(send(low(total[1]), "xh", 1))


def gather_wid(value):
    own = jnp.stack([value, send(value, "xh", 1)])
    after = send(own, "z", -1)
    before = send(own, "z", 1)
    far = jnp.stack([send(after[0], "z", -1), send(before[1], "z", 1)])
    return [own, after, far, before]


def local(tokens, up_weight, down_weight, cotangent):
    width = tokens.shape[-1]
    hidden = up_weight.shape[-1]
    tok_all = gather_groups(relative(tokens)).reshape(4, 256, width)
    cot_all = gather_groups(relative(cotangent)).reshape(4, 256, width)
    order = (2, 1, 3, 0)
    pre_terms = [None] * 4
    grad_terms = [None] * 4
    for d in order:
        pre_terms[d] = low(contract(tok_all[d], up_weight, 1, 0)).reshape(2, 128, hidden)
    for d in order:
        grad_terms[d] = low(contract(cot_all[d], down_weight, 1, 1)).reshape(2, 128, hidden)
    preact = scatter_wid(pre_terms)
    act_grad = scatter_wid(grad_terms)
    activated, derivative = gelu_parts(preact)
    act = [part.reshape(256, hidden) for part in gather_wid(low(activated))]
    hgrad = [part.reshape(256, hidden) for part in gather_wid(low(act_grad * derivative))]
    out_terms = jnp.stack([low(contract(part, down_weight, 1, 0)) for part in act])
    layer_out = scatter_groups(out_terms.reshape(4, 2, 16, 8, width))
    back_terms = jnp.stack([low(contract(part, up_weight, 1, 1)) for part in hgrad])
    tokens_grad = scatter_groups(back_terms.reshape(4, 2, 16, 8, width))
    grad_scale = 1.0 / math.sqrt(1024.0)
    act_all = jnp.concatenate(act)
    hgrad_all = jnp.concatenate(hgrad)
    down_grad = low(contract(act_all, cot_all.reshape(1024, width), 0, 0) * grad_scale)
    up_grad = low(contract(tok_all.reshape(1024, width), hgrad_all, 0, 0) * grad_scale)
    return (absolute(low(layer_out)), absolute(low(tokens_grad)), up_grad, down_grad)


def solution(mesh):
    fine = Mesh(mesh.devices.reshape(2, 2, 4, 2, 4), AXES)
    rows = P(("xl", "c", "y"), ("z", "xh"))
    up_spec = P(("z", "xh"), ("y", "xl", "c"))
    down_spec = P(("y", "xl", "c"), ("z", "xh"))
    return jax.shard_map(
        local,
        mesh=fine,
        in_specs=(rows, up_spec, down_spec, rows),
        out_specs=(rows, rows, up_spec, down_spec),
        check_vma=False,
    )
```

time: 538 us -> 208 us (0.39)
  waiting for transfers between devices: 479 us -> 110 us
  starting transfers between devices: 0.5 us -> 60.7 us
  matrix products: 36.8 us -> 20.5 us
  between operations: 14.1 us -> 1.39 us
  other arithmetic: 2.57 us -> 8.03 us
    reduce_scatter x4 -> x0, waiting for transfers between devices: 265 us -> none  [the longest x1 81.9 us: local(): preact = lax.psum_scatter(pre_terms, 'wid', scatter_dimension=0, tiled=True)]
    all_gather x4 -> x0, waiting for transfers between devices: 212 us -> none  [the longest x1 61.1 us: local(): lax.all_gather(activated.astype(jnp.bfloat16), 'wid', axis=0, tiled=True)]
    ppermute x0 -> x40, waiting for transfers between devices: none -> 110 us  [send(): lax.ppermute(value, axis, [(i, (i + step) % count) for i in range(count)])]
    ppermute x0 -> x40, starting transfers between devices: none -> 60.7 us  [send(): lax.ppermute(value, axis, [(i, (i + step) % count) for i in range(count)])]
    dot_general x6 -> x18, matrix products: 36.8 us -> 20.5 us  [contract(): lax.dot_general(left, right, (((left_dim,), (right_dim,)), ((), ())), pre...]
  transfers between devices with their start and end apart: 8 -> 40, of which waited for: 8 -> 20; matrix products, arithmetic and copies ran while one was open for 8% -> 13% of each run, Pallas kernels for 0% -> 0%
where the time goes in v2:
time: 208 us; the launch traced here: 207 us
  waiting for transfers between devices  110 us (53%)
  starting transfers between devices  60.7 us (29%)
  matrix products  20.5 us (10%)
  other arithmetic  8.03 us (4%)
  local copies, waits for them, and re-layouts  6.6 us (3%)
    ppermute x40, waiting for transfers between devices, send(): lax.ppermute(value, axis, [(i, (i + step) % count) for i in range(count)])  110 us
    ppermute x40, starting transfers between devices, send(): lax.ppermute(value, axis, [(i, (i + step) % count) for i in range(count)])  60.7 us
    dot_general x18, matrix products, contract(): lax.dot_general(left, right, (((left_dim,), (right_dim,)), ((), ())), pre...  20.5 us
    unnamed x24, local copies, waits for them, and re-layouts  5.6 us
  transfers between devices with their start and end apart: 40, of which 20 were waited for; matrix products, arithmetic and copies ran while one was open for 13% of the time, Pallas kernels for 0%

profile of v2, /device:TPU:0, one launch (start us, length us, event | category | flops | bytes accessed | tf_op | source)
XLA Modules:
  0.0 206.8 jit_solution(8033208069681951346)
XLA Ops:
  6.7 3.0 %collective-permute-start.21 = (bf16[4,2,2,8,768]{4,3,2,1,0:T(8,128)(2,1)S(1)}, bf16[4,2,2,8,768]{4,3,2,1,0:T(8,128)(2,1)S(1)}, u32[]{:S(2)}, u32[]{:S(2)}) collective-permute-start(bf16[4,2,2,8,768]{4,3,2,1,0:T(8,128)(2,1)S(1)} %pad_maximum_fusion.11), channel_id=1, source_target_pairs={{0,3},{1,0},{2,1},{3,2},{4,7},{5,4},{6,5},{7,6},{8,11},{9,8},{10,9... | collective-permute-start | bytes 589832 | tf_op jit(solution)/shard_map/ppermute | solution.py:43
  12.0 5.1 %collective-permute-done.21 = bf16[4,2,2,8,768]{4,3,2,1,0:T(8,128)(2,1)S(1)} collective-permute-done((bf16[4,2,2,8,768]{4,3,2,1,0:T(8,128)(2,1)S(1)}, bf16[4,2,2,8,768]{4,3,2,1,0:T(8,128)(2,1)S(1)}, u32[]{:S(2)}, u32[]{:S(2)}) %collective-permute-start.21) | collective-permute-done | bytes 196640 | tf_op jit(solution)/shard_map/ppermute | solution.py:43
  17.2 2.3 %collective-permute-done.22 = bf16[4,2,2,8,768]{4,3,2,1,0:T(8,128)(2,1)S(1)} collective-permute-done((bf16[4,2,2,8,768]{4,3,2,1,0:T(8,128)(2,1)S(1)}, bf16[4,2,2,8,768]{4,3,2,1,0:T(8,128)(2,1)S(1)}, u32[]{:S(2)}, u32[]{:S(2)}) %collective-permute-start.22) | collective-permute-done | bytes 196640 | tf_op jit(solution)/shard_map/ppermute | solution.py:43
  23.4 5.0 %collective-permute-done.1 = bf16[4,2,2,8,768]{4,3,2,1,0:T(8,128)(2,1)S(1)} collective-permute-done((bf16[4,2,2,8,768]{4,3,2,1,0:T(8,128)(2,1)S(1)}, bf16[4,2,2,8,768]{4,3,2,1,0:T(8,128)(2,1)S(1)}, u32[]{:S(2)}, u32[]{:S(2)}) %collective-permute-start.1) | collective-permute-done | bytes 196640 | tf_op jit(solution)/shard_map/ppermute | solution.py:43
  28.4 4.3 %collective-permute-done.2 = bf16[4,2,2,8,768]{4,3,2,1,0:T(8,128)(2,1)S(1)} collective-permute-done((bf16[4,2,2,8,768]{4,3,2,1,0:T(8,128)(2,1)S(1)}, bf16[4,2,2,8,768]{4,3,2,1,0:T(8,128)(2,1)S(1)}, u32[]{:S(2)}, u32[]{:S(2)}) %collective-permute-start.2) | collective-permute-done | bytes 196640 | tf_op jit(solution)/shard_map/ppermute | solution.py:43
  38.7 2.2 %collective-permute-start.27 = (bf16[128,1536]{1,0:T(8,128)(2,1)S(1)}, bf16[128,1536]{1,0:T(8,128)(2,1)S(1)}, u32[]{:S(2)}, u32[]{:S(2)}) collective-permute-start(bf16[128,1536]{1,0:T(8,128)(2,1)S(1)} %get-tuple-element.22), channel_id=1, source_target_pairs={{0,24},{8,0},{16,8},{24,16},{1,25},{9,1},{17,9},{25,17},{2,26},{10... | collective-permute-start | bytes 1179656 | tf_op jit(solution)/shard_map/ppermute | solution.py:43
  47.5 3.2 %collective-permute-start.7 = (bf16[128,1536]{1,0:T(8,128)(2,1)S(1)}, bf16[128,1536]{1,0:T(8,128)(2,1)S(1)}, u32[]{:S(2)}, u32[]{:S(2)}) collective-permute-start(bf16[128,1536]{1,0:T(8,128)(2,1)S(1)} %get-tuple-element.27), channel_id=1, source_target_pairs={{0,24},{8,0},{16,8},{24,16},{1,25},{9,1},{17,9},{25,17},{2,26},{10... | collective-permute-start | bytes 1179656 | tf_op jit(solution)/shard_map/ppermute | solution.py:43
  51.7 2.2 %collective-permute-start.28 = (bf16[2,128,1536]{2,1,0:T(8,128)(2,1)S(1)}, bf16[2,128,1536]{2,1,0:T(8,128)(2,1)S(1)}, u32[]{:S(2)}, u32[]{:S(2)}) collective-permute-start(bf16[2,128,1536]{2,1,0:T(8,128)(2,1)S(1)} %pad_maximum_fusion.7), channel_id=1, source_target_pairs={{0,24},{8,0},{16,8},{24,16},{1,25},{9,1},{17,9},{25,17},{2,26},{10... | collective-permute-start | bytes 2359304 | tf_op jit(solution)/shard_map/ppermute | solution.py:43
  54.1 6.1 %collective-permute-done.7 = bf16[128,1536]{1,0:T(8,128)(2,1)S(1)} collective-permute-done((bf16[128,1536]{1,0:T(8,128)(2,1)S(1)}, bf16[128,1536]{1,0:T(8,128)(2,1)S(1)}, u32[]{:S(2)}, u32[]{:S(2)}) %collective-permute-start.7) | collective-permute-done | bytes 393248 | tf_op jit(solution)/shard_map/ppermute | solution.py:43
  60.4 3.8 %collective-permute-start.8 = (bf16[2,128,1536]{2,1,0:T(8,128)(2,1)S(1)}, bf16[2,128,1536]{2,1,0:T(8,128)(2,1)S(1)}, u32[]{:S(2)}, u32[]{:S(2)}) collective-permute-start(bf16[2,128,1536]{2,1,0:T(8,128)(2,1)S(1)} %pad_maximum_fusion.3), channel_id=1, source_target_pairs={{0,24},{8,0},{16,8},{24,16},{1,25},{9,1},{17,9},{25,17},{2,26},{10... | collective-permute-start | bytes 2359304 | tf_op jit(solution)/shard_map/ppermute | solution.py:43
  64.6 12.4 %collective-permute-done.28 = bf16[2,128,1536]{2,1,0:T(8,128)(2,1)S(1)} collective-permute-done((bf16[2,128,1536]{2,1,0:T(8,128)(2,1)S(1)}, bf16[2,128,1536]{2,1,0:T(8,128)(2,1)S(1)}, u32[]{:S(2)}, u32[]{:S(2)}) %collective-permute-start.28) | collective-permute-done | bytes 786464 | tf_op jit(solution)/shard_map/ppermute | solution.py:43
  77.8 3.3 %collective-permute-start.29 = (bf16[128,1536]{1,0:T(8,128)(2,1)S(1)}, bf16[128,1536]{1,0:T(8,128)(2,1)S(1)}, u32[]{:S(2)}, u32[]{:S(2)}) collective-permute-start(bf16[128,1536]{1,0:T(8,128)(2,1)S(1)} %fusion.30), channel_id=1, source_target_pairs={{0,4},{4,0},{1,5},{5,1},{2,6},{6,2},{3,7},{7,3},{8,12},{12,8},{9,1... | collective-permute-start | bytes 1179656 | tf_op jit(solution)/shard_map/ppermute | solution.py:43
  81.1 11.8 %collective-permute-done.8 = bf16[2,128,1536]{2,1,0:T(8,128)(2,1)S(1)} collective-permute-done((bf16[2,128,1536]{2,1,0:T(8,128)(2,1)S(1)}, bf16[2,128,1536]{2,1,0:T(8,128)(2,1)S(1)}, u32[]{:S(2)}, u32[]{:S(2)}) %collective-permute-start.8) | collective-permute-done | bytes 786464 | tf_op jit(solution)/shard_map/ppermute | solution.py:43
  93.9 3.3 %collective-permute-start.9 = (bf16[128,1536]{1,0:T(8,128)(2,1)S(1)}, bf16[128,1536]{1,0:T(8,128)(2,1)S(1)}, u32[]{:S(2)}, u32[]{:S(2)}) collective-permute-start(bf16[128,1536]{1,0:T(8,128)(2,1)S(1)} %fusion.29), channel_id=1, source_target_pairs={{0,4},{4,0},{1,5},{5,1},{2,6},{6,2},{3,7},{7,3},{8,12},{12,8},{9,1... | collective-permute-start | bytes 1179656 | tf_op jit(solution)/shard_map/ppermute | solution.py:43
  97.2 8.7 %collective-permute-done.9 = bf16[128,1536]{1,0:T(8,128)(2,1)S(1)} collective-permute-done((bf16[128,1536]{1,0:T(8,128)(2,1)S(1)}, bf16[128,1536]{1,0:T(8,128)(2,1)S(1)}, u32[]{:S(2)}, u32[]{:S(2)}) %collective-permute-start.9) | collective-permute-done | bytes 393248 | tf_op jit(solution)/shard_map/ppermute | solution.py:43
  106.5 3.3 %collective-permute-start.10 = (bf16[128,1536]{1,0:T(8,128)(2,1)S(1)}, bf16[128,1536]{1,0:T(8,128)(2,1)}, u32[]{:S(2)}, u32[]{:S(2)}) collective-permute-start(bf16[128,1536]{1,0:T(8,128)(2,1)S(1)} %get-tuple-element.9), channel_id=1, source_target_pairs={{0,4},{4,0},{1,5},{5,1},{2,6},{6,2},{3,7},{7,3},{8,12},{12,8},{9,1... | collective-permute-start | bytes 1179656 | tf_op jit(solution)/shard_map/ppermute | solution.py:43
  110.1 10.1 %collective-permute-done.10 = bf16[128,1536]{1,0:T(8,128)(2,1)} collective-permute-done((bf16[128,1536]{1,0:T(8,128)(2,1)S(1)}, bf16[128,1536]{1,0:T(8,128)(2,1)}, u32[]{:S(2)}, u32[]{:S(2)}) %collective-permute-start.10) | collective-permute-done | bytes 393248 | tf_op jit(solution)/shard_map/ppermute | solution.py:43
  121.8 3.1 %collective-permute-start.11 = (bf16[2,128,1536]{2,1,0:T(8,128)(2,1)S(1)}, bf16[2,128,1536]{2,1,0:T(8,128)(2,1)S(1)}, u32[]{:S(2)}, u32[]{:S(2)}) collective-permute-start(bf16[2,128,1536]{2,1,0:T(8,128)(2,1)S(1)} %pad_maximum_fusion.4), channel_id=1, source_target_pairs={{0,24},{8,0},{16,8},{24,16},{1,25},{9,1},{17,9},{25,17},{2,26},{10... | collective-permute-start | bytes 2359304 | tf_op jit(solution)/shard_map/ppermute | solution.py:43
  126.2 3.2 %collective-permute-start.31 = (bf16[2,128,1536]{2,1,0:T(8,128)(2,1)S(1)}, bf16[2,128,1536]{2,1,0:T(8,128)(2,1)S(1)}, u32[]{:S(2)}, u32[]{:S(2)}) collective-permute-start(bf16[2,128,1536]{2,1,0:T(8,128)(2,1)S(1)} %pad_maximum_fusion.8), channel_id=1, source_target_pairs={{0,24},{8,0},{16,8},{24,16},{1,25},{9,1},{17,9},{25,17},{2,26},{10... | collective-permute-start | bytes 2359304 | tf_op jit(solution)/shard_map/ppermute | solution.py:43
  131.0 12.3 %collective-permute-done.13 = bf16[2,128,1536]{2,1,0:T(8,128)(2,1)S(1)} collective-permute-done((bf16[2,128,1536]{2,1,0:T(8,128)(2,1)S(1)}, bf16[2,128,1536]{2,1,0:T(8,128)(2,1)S(1)}, u32[]{:S(2)}, u32[]{:S(2)}) %collective-permute-start.13) | collective-permute-done | bytes 786464 | tf_op jit(solution)/shard_map/ppermute | solution.py:43
  143.4 3.3 %collective-permute-start.12 = (bf16[128,1536]{1,0:T(8,128)(2,1)S(1)}, bf16[128,1536]{1,0:T(8,128)(2,1)S(1)}, u32[]{:S(2)}, u32[]{:S(2)}) collective-permute-start(bf16[128,1536]{1,0:T(8,128)(2,1)S(1)} %slice_bitcast_fusion.7), channel_id=1, source_target_pairs={{0,24},{8,0},{16,8},{24,16},{1,25},{9,1},{17,9},{25,17},{2,26},{10... | collective-permute-start | bytes 1179656 | tf_op jit(solution)/shard_map/ppermute | solution.py:43
  146.7 13.4 %collective-permute-done.33 = bf16[2,128,1536]{2,1,0:T(8,128)(2,1)S(1)} collective-permute-done((bf16[2,128,1536]{2,1,0:T(8,128)(2,1)S(1)}, bf16[2,128,1536]{2,1,0:T(8,128)(2,1)S(1)}, u32[]{:S(2)}, u32[]{:S(2)}) %collective-permute-start.33) | collective-permute-done | bytes 786464 | tf_op jit(solution)/shard_map/ppermute | solution.py:43
  162.6 3.3 %collective-permute-start.32 = (bf16[128,1536]{1,0:T(8,128)(2,1)S(1)}, bf16[128,1536]{1,0:T(8,128)(2,1)S(1)}, u32[]{:S(2)}, u32[]{:S(2)}) collective-permute-start(bf16[128,1536]{1,0:T(8,128)(2,1)S(1)} %slice_bitcast_fusion.3), channel_id=1, source_target_pairs={{0,24},{8,0},{16,8},{24,16},{1,25},{9,1},{17,9},{25,17},{2,26},{10... | collective-permute-start | bytes 1179656 | tf_op jit(solution)/shard_map/ppermute | solution.py:43
  169.3 3.9 %multiply_convert_fusion = bf16[1536,768]{1,0:T(8,128)(2,1)} fusion(bf16[1024,768]{1,0:T(8,128)(2,1)S(1)} %bitcast.142, bf16[256,1536]{1,0:T(8,128)(2,1)S(1)} %bitcast.182, bf16[256,1536]{1,0:T(8,128)(2,1)S(1)} %bitcast.151, bf16[256,1536]{1,0:T(8,128)(2,1)S(1)} %bitcast.184, bf16[256,1536]{1,0:T(8,128)(2,1)S(1)} %bitcast.149), kind=kOutput, calls=%fused_computation | convolution fusion | flops 2430861312 | bytes 7077888 | tf_op jit(solution)/shard_map/dot_general | solution.py:25
  175.7 3.9 %multiply_convert_fusion.1 = bf16[768,1536]{1,0:T(8,128)(2,1)} fusion(bf16[1024,768]{1,0:T(8,128)(2,1)S(1)} %bitcast.143, bf16[256,1536]{1,0:T(8,128)(2,1)S(1)} %bitcast.178, bf16[256,1536]{1,0:T(8,128)(2,1)S(1)} %bitcast.153, bf16[256,1536]{1,0:T(8,128)(2,1)S(1)} %bitcast.180, bf16[256,1536]{1,0:T(8,128)(2,1)S(1)} %bitcast.147), kind=kOutput, calls=%fused_computation.1 | convolution fusion | flops 2430861312 | bytes 7077888 | tf_op jit(solution)/shard_map/dot_general | solution.py:25
  180.0 3.2 %collective-permute-start.18 = (bf16[4,2,2,8,768]{4,3,2,1,0:T(8,128)(2,1)S(1)}, bf16[4,2,2,8,768]{4,3,2,1,0:T(8,128)(2,1)S(1)}, u32[]{:S(2)}, u32[]{:S(2)}) collective-permute-start(bf16[4,2,2,8,768]{4,3,2,1,0:T(8,128)(2,1)S(1)} %get-tuple-element.24), channel_id=1, source_target_pairs={{0,3},{1,0},{2,1},{3,2},{4,7},{5,4},{6,5},{7,6},{8,11},{9,8},{10,9... | collective-permute-start | bytes 589832 | tf_op jit(solution)/shard_map/ppermute | solution.py:43
  184.4 3.0 %collective-permute-start.38 = (bf16[4,2,2,8,768]{4,3,2,1,0:T(8,128)(2,1)S(1)}, bf16[4,2,2,8,768]{4,3,2,1,0:T(8,128)(2,1)S(1)}, u32[]{:S(2)}, u32[]{:S(2)}) collective-permute-start(bf16[4,2,2,8,768]{4,3,2,1,0:T(8,128)(2,1)S(1)} %get-tuple-element.19), channel_id=1, source_target_pairs={{0,3},{1,0},{2,1},{3,2},{4,7},{5,4},{6,5},{7,6},{8,11},{9,8},{10,9... | collective-permute-start | bytes 589832 | tf_op jit(solution)/shard_map/ppermute | solution.py:43
  187.5 5.2 %collective-permute-done.16 = bf16[4,2,2,8,768]{4,3,2,1,0:T(8,128)(2,1)S(1)} collective-permute-done((bf16[4,2,2,8,768]{4,3,2,1,0:T(8,128)(2,1)S(1)}, bf16[4,2,2,8,768]{4,3,2,1,0:T(8,128)(2,1)S(1)}, u32[]{:S(2)}, u32[]{:S(2)}) %collective-permute-start.16) | collective-permute-done | bytes 196640 | tf_op jit(solution)/shard_map/ppermute | solution.py:43
  192.8 2.8 %collective-permute-start.19 = (bf16[4,2,8,768]{3,2,1,0:T(8,128)(2,1)S(1)}, bf16[4,2,8,768]{3,2,1,0:T(8,128)(2,1)S(1)}, u32[]{:S(2)}, u32[]{:S(2)}) collective-permute-start(bf16[4,2,8,768]{3,2,1,0:T(8,128)(2,1)S(1)} %slice_bitcast_fusion.12), channel_id=1, source_target_pairs={{0,64},{64,0},{1,65},{65,1},{2,66},{66,2},{3,67},{67,3},{4,68},{68... | collective-permute-start | bytes 294920 | tf_op jit(solution)/shard_map/ppermute | solution.py:43
  195.6 4.5 %collective-permute-done.36 = bf16[4,2,2,8,768]{4,3,2,1,0:T(8,128)(2,1)S(1)} collective-permute-done((bf16[4,2,2,8,768]{4,3,2,1,0:T(8,128)(2,1)S(1)}, bf16[4,2,2,8,768]{4,3,2,1,0:T(8,128)(2,1)S(1)}, u32[]{:S(2)}, u32[]{:S(2)}) %collective-permute-start.36) | collective-permute-done | bytes 196640 | tf_op jit(solution)/shard_map/ppermute | solution.py:43
  200.3 2.5 %collective-permute-start.39 = (bf16[4,2,8,768]{3,2,1,0:T(8,128)(2,1)S(1)}, bf16[4,2,8,768]{3,2,1,0:T(8,128)(2,1)S(1)}, u32[]{:S(2)}, u32[]{:S(2)}) collective-permute-start(bf16[4,2,8,768]{3,2,1,0:T(8,128)(2,1)S(1)} %slice_bitcast_fusion.10), channel_id=1, source_target_pairs={{0,64},{64,0},{1,65},{65,1},{2,66},{66,2},{3,67},{67,3},{4,68},{68... | collective-permute-start | bytes 294920 | tf_op jit(solution)/shard_map/ppermute | solution.py:43
  202.8 2.6 %collective-permute-done.39 = bf16[4,2,8,768]{3,2,1,0:T(8,128)(2,1)S(1)} collective-permute-done((bf16[4,2,8,768]{3,2,1,0:T(8,128)(2,1)S(1)}, bf16[4,2,8,768]{3,2,1,0:T(8,128)(2,1)S(1)}, u32[]{:S(2)}, u32[]{:S(2)}) %collective-permute-start.39) | collective-permute-done | bytes 98336 | tf_op jit(solution)/shard_map/ppermute | solution.py:43
  (146 shorter events, 45.2 us)
Async XLA Ops:
  4.5 16.1 %collective-permute-start = (bf16[4,2,1,8,768]{4,3,2,1,0:T(8,128)(2,1)S(1)}, bf16[4,2,1,8,768]{4,3,2,1,0:T(8,128)(2,1)S(1)}, u32[]{:S(2)}, u32[]{:S(2)}) collective-permute-start(bf16[4,2,1,8,768]{4,3,2,1,0:T(8,128)(2,1)S(1)} %get-tuple-element.7), channel_id=1, source_target_pairs={{0,64},{64,0},{1,65},{65,1},{2,66},{66,2},{3,67},{67,3},{4,68},{68... | collective-permute-start | bytes 294920 | tf_op jit(solution)/shard_map/ppermute | solution.py:43
  6.7 10.5 %collective-permute-start.21 = (bf16[4,2,2,8,768]{4,3,2,1,0:T(8,128)(2,1)S(1)}, bf16[4,2,2,8,768]{4,3,2,1,0:T(8,128)(2,1)S(1)}, u32[]{:S(2)}, u32[]{:S(2)}) collective-permute-start(bf16[4,2,2,8,768]{4,3,2,1,0:T(8,128)(2,1)S(1)} %pad_maximum_fusion.11), channel_id=1, source_target_pairs={{0,3},{1,0},{2,1},{3,2},{4,7},{5,4},{6,5},{7,6},{8,11},{9,8},{10,9... | collective-permute-start | bytes 589832 | tf_op jit(solution)/shard_map/ppermute | solution.py:43
  9.7 10.7 %collective-permute-start.23 = (bf16[4,2,2,8,768]{4,3,2,1,0:T(8,128)(2,1)S(1)}, bf16[4,2,2,8,768]{4,3,2,1,0:T(8,128)(2,1)S(1)}, u32[]{:S(2)}, u32[]{:S(2)}) collective-permute-start(bf16[4,2,2,8,768]{4,3,2,1,0:T(8,128)(2,1)S(1)} %pad_maximum_fusion.11), channel_id=1, source_target_pairs={{0,1},{1,2},{2,3},{3,0},{4,5},{5,6},{6,7},{7,4},{8,9},{9,10},{10,1... | collective-permute-start | bytes 589832 | tf_op jit(solution)/shard_map/ppermute | solution.py:43
  20.4 13.3 %collective-permute-start.24 = (bf16[4,2,8,8,768]{4,3,2,1,0:T(8,128)(2,1)S(1)}, bf16[4,2,8,8,768]{4,3,2,1,0:T(8,128)(2,1)S(1)}, u32[]{:S(2)}, u32[]{:S(2)}) collective-permute-start(bf16[4,2,8,8,768]{4,3,2,1,0:T(8,128)(2,1)S(1)} %get-tuple-element.28), channel_id=1, source_target_pairs={{0,32},{32,0},{1,33},{33,1},{2,34},{34,2},{3,35},{35,3},{4,36},{36... | collective-permute-start | bytes 2359304 | tf_op jit(solution)/shard_map/ppermute | solution.py:43
  21.1 12.5 %collective-permute-start.3 = (bf16[4,2,2,8,768]{4,3,2,1,0:T(8,128)(2,1)S(1)}, bf16[4,2,2,8,768]{4,3,2,1,0:T(8,128)(2,1)S(1)}, u32[]{:S(2)}, u32[]{:S(2)}) collective-permute-start(bf16[4,2,2,8,768]{4,3,2,1,0:T(8,128)(2,1)S(1)} %pad_maximum_fusion.10), channel_id=1, source_target_pairs={{0,1},{1,2},{2,3},{3,0},{4,5},{5,6},{6,7},{7,4},{8,9},{9,10},{10,1... | collective-permute-start | bytes 589832 | tf_op jit(solution)/shard_map/ppermute | solution.py:43
  22.7 9.9 %collective-permute-start.2 = (bf16[4,2,2,8,768]{4,3,2,1,0:T(8,128)(2,1)S(1)}, bf16[4,2,2,8,768]{4,3,2,1,0:T(8,128)(2,1)S(1)}, u32[]{:S(2)}, u32[]{:S(2)}) collective-permute-start(bf16[4,2,2,8,768]{4,3,2,1,0:T(8,128)(2,1)S(1)} %pad_maximum_fusion.10), channel_id=1, source_target_pairs={{0,2},{1,3},{2,0},{3,1},{4,6},{5,7},{6,4},{7,5},{8,10},{9,11},{10,... | collective-permute-start | bytes 589832 | tf_op jit(solution)/shard_map/ppermute | solution.py:43
  36.7 17.2 %collective-permute-start.25 = (bf16[128,1536]{1,0:T(8,128)(2,1)S(1)}, bf16[128,1536]{1,0:T(8,128)(2,1)S(1)}, u32[]{:S(2)}, u32[]{:S(2)}) collective-permute-start(bf16[128,1536]{1,0:T(8,128)(2,1)S(1)} %get-tuple-element.21), channel_id=1, source_target_pairs={{0,8},{8,16},{16,24},{24,0},{1,9},{9,17},{17,25},{25,1},{2,10},{10... | collective-permute-start | bytes 1179656 | tf_op jit(solution)/shard_map/ppermute | solution.py:43
  38.7 12.8 %collective-permute-start.27 = (bf16[128,1536]{1,0:T(8,128)(2,1)S(1)}, bf16[128,1536]{1,0:T(8,128)(2,1)S(1)}, u32[]{:S(2)}, u32[]{:S(2)}) collective-permute-start(bf16[128,1536]{1,0:T(8,128)(2,1)S(1)} %get-tuple-element.22), channel_id=1, source_target_pairs={{0,24},{8,0},{16,8},{24,16},{1,25},{9,1},{17,9},{25,17},{2,26},{10... | collective-permute-start | bytes 1179656 | tf_op jit(solution)/shard_map/ppermute | solution.py:43
  47.4 16.8 %collective-permute-start.5 = (bf16[128,1536]{1,0:T(8,128)(2,1)S(1)}, bf16[128,1536]{1,0:T(8,128)(2,1)S(1)}, u32[]{:S(2)}, u32[]{:S(2)}) collective-permute-start(bf16[128,1536]{1,0:T(8,128)(2,1)S(1)} %get-tuple-element.26), channel_id=1, source_target_pairs={{0,8},{8,16},{16,24},{24,0},{1,9},{9,17},{17,25},{25,1},{2,10},{10... | collective-permute-start | bytes 1179656 | tf_op jit(solution)/shard_map/ppermute | solution.py:43
  47.5 12.7 %collective-permute-start.7 = (bf16[128,1536]{1,0:T(8,128)(2,1)S(1)}, bf16[128,1536]{1,0:T(8,128)(2,1)S(1)}, u32[]{:S(2)}, u32[]{:S(2)}) collective-permute-start(bf16[128,1536]{1,0:T(8,128)(2,1)S(1)} %get-tuple-element.27), channel_id=1, source_target_pairs={{0,24},{8,0},{16,8},{24,16},{1,25},{9,1},{17,9},{25,17},{2,26},{10... | collective-permute-start | bytes 1179656 | tf_op jit(solution)/shard_map/ppermute | solution.py:43
  51.7 25.4 %collective-permute-start.28 = (bf16[2,128,1536]{2,1,0:T(8,128)(2,1)S(1)}, bf16[2,128,1536]{2,1,0:T(8,128)(2,1)S(1)}, u32[]{:S(2)}, u32[]{:S(2)}) collective-permute-start(bf16[2,128,1536]{2,1,0:T(8,128)(2,1)S(1)} %pad_maximum_fusion.7), channel_id=1, source_target_pairs={{0,24},{8,0},{16,8},{24,16},{1,25},{9,1},{17,9},{25,17},{2,26},{10... | collective-permute-start | bytes 2359304 | tf_op jit(solution)/shard_map/ppermute | solution.py:43
  54.1 23.4 %collective-permute-start.26 = (bf16[2,128,1536]{2,1,0:T(8,128)(2,1)S(1)}, bf16[2,128,1536]{2,1,0:T(8,128)(2,1)S(1)}, u32[]{:S(2)}, u32[]{:S(2)}) collective-permute-start(bf16[2,128,1536]{2,1,0:T(8,128)(2,1)S(1)} %pad_maximum_fusion.6), channel_id=1, source_target_pairs={{0,8},{8,16},{16,24},{24,0},{1,9},{9,17},{17,25},{25,1},{2,10},{10... | collective-permute-start | bytes 2359304 | tf_op jit(solution)/shard_map/ppermute | solution.py:43
  60.4 32.5 %collective-permute-start.8 = (bf16[2,128,1536]{2,1,0:T(8,128)(2,1)S(1)}, bf16[2,128,1536]{2,1,0:T(8,128)(2,1)S(1)}, u32[]{:S(2)}, u32[]{:S(2)}) collective-permute-start(bf16[2,128,1536]{2,1,0:T(8,128)(2,1)S(1)} %pad_maximum_fusion.3), channel_id=1, source_target_pairs={{0,24},{8,0},{16,8},{24,16},{1,25},{9,1},{17,9},{25,17},{2,26},{10... | collective-permute-start | bytes 2359304 | tf_op jit(solution)/shard_map/ppermute | solution.py:43
  64.3 29.2 %collective-permute-start.6 = (bf16[2,128,1536]{2,1,0:T(8,128)(2,1)S(1)}, bf16[2,128,1536]{2,1,0:T(8,128)(2,1)S(1)}, u32[]{:S(2)}, u32[]{:S(2)}) collective-permute-start(bf16[2,128,1536]{2,1,0:T(8,128)(2,1)S(1)} %pad_maximum_fusion.2), channel_id=1, source_target_pairs={{0,8},{8,16},{16,24},{24,0},{1,9},{9,17},{17,25},{25,1},{2,10},{10... | collective-permute-start | bytes 2359304 | tf_op jit(solution)/shard_map/ppermute | solution.py:43
  77.8 19.4 %collective-permute-start.29 = (bf16[128,1536]{1,0:T(8,128)(2,1)S(1)}, bf16[128,1536]{1,0:T(8,128)(2,1)S(1)}, u32[]{:S(2)}, u32[]{:S(2)}) collective-permute-start(bf16[128,1536]{1,0:T(8,128)(2,1)S(1)} %fusion.30), channel_id=1, source_target_pairs={{0,4},{4,0},{1,5},{5,1},{2,6},{6,2},{3,7},{7,3},{8,12},{12,8},{9,1... | collective-permute-start | bytes 1179656 | tf_op jit(solution)/shard_map/ppermute | solution.py:43
  93.9 12.0 %collective-permute-start.9 = (bf16[128,1536]{1,0:T(8,128)(2,1)S(1)}, bf16[128,1536]{1,0:T(8,128)(2,1)S(1)}, u32[]{:S(2)}, u32[]{:S(2)}) collective-permute-start(bf16[128,1536]{1,0:T(8,128)(2,1)S(1)} %fusion.29), channel_id=1, source_target_pairs={{0,4},{4,0},{1,5},{5,1},{2,6},{6,2},{3,7},{7,3},{8,12},{12,8},{9,1... | collective-permute-start | bytes 1179656 | tf_op jit(solution)/shard_map/ppermute | solution.py:43
  106.5 13.7 %collective-permute-start.10 = (bf16[128,1536]{1,0:T(8,128)(2,1)S(1)}, bf16[128,1536]{1,0:T(8,128)(2,1)}, u32[]{:S(2)}, u32[]{:S(2)}) collective-permute-start(bf16[128,1536]{1,0:T(8,128)(2,1)S(1)} %get-tuple-element.9), channel_id=1, source_target_pairs={{0,4},{4,0},{1,5},{5,1},{2,6},{6,2},{3,7},{7,3},{8,12},{12,8},{9,1... | collective-permute-start | bytes 1179656 | tf_op jit(solution)/shard_map/ppermute | solution.py:43
  109.8 16.2 %collective-permute-start.30 = (bf16[128,1536]{1,0:T(8,128)(2,1)S(1)}, bf16[128,1536]{1,0:T(8,128)(2,1)S(1)}, u32[]{:S(2)}, u32[]{:S(2)}) collective-permute-start(bf16[128,1536]{1,0:T(8,128)(2,1)S(1)} %get-tuple-element.8), channel_id=1, source_target_pairs={{0,4},{4,0},{1,5},{5,1},{2,6},{6,2},{3,7},{7,3},{8,12},{12,8},{9,1... | collective-permute-start | bytes 1179656 | tf_op jit(solution)/shard_map/ppermute | solution.py:43
  121.5 21.8 %collective-permute-start.13 = (bf16[2,128,1536]{2,1,0:T(8,128)(2,1)S(1)}, bf16[2,128,1536]{2,1,0:T(8,128)(2,1)S(1)}, u32[]{:S(2)}, u32[]{:S(2)}) collective-permute-start(bf16[2,128,1536]{2,1,0:T(8,128)(2,1)S(1)} %pad_maximum_fusion.4), channel_id=1, source_target_pairs={{0,8},{8,16},{16,24},{24,0},{1,9},{9,17},{17,25},{25,1},{2,10},{10... | collective-permute-start | bytes 2359304 | tf_op jit(solution)/shard_map/ppermute | solution.py:43
  121.8 21.6 %collective-permute-start.11 = (bf16[2,128,1536]{2,1,0:T(8,128)(2,1)S(1)}, bf16[2,128,1536]{2,1,0:T(8,128)(2,1)S(1)}, u32[]{:S(2)}, u32[]{:S(2)}) collective-permute-start(bf16[2,128,1536]{2,1,0:T(8,128)(2,1)S(1)} %pad_maximum_fusion.4), channel_id=1, source_target_pairs={{0,24},{8,0},{16,8},{24,16},{1,25},{9,1},{17,9},{25,17},{2,26},{10... | collective-permute-start | bytes 2359304 | tf_op jit(solution)/shard_map/ppermute | solution.py:43
  126.1 34.0 %collective-permute-start.33 = (bf16[2,128,1536]{2,1,0:T(8,128)(2,1)S(1)}, bf16[2,128,1536]{2,1,0:T(8,128)(2,1)S(1)}, u32[]{:S(2)}, u32[]{:S(2)}) collective-permute-start(bf16[2,128,1536]{2,1,0:T(8,128)(2,1)S(1)} %pad_maximum_fusion.8), channel_id=1, source_target_pairs={{0,8},{8,16},{16,24},{24,0},{1,9},{9,17},{17,25},{25,1},{2,10},{10... | collective-permute-start | bytes 2359304 | tf_op jit(solution)/shard_map/ppermute | solution.py:43
  126.2 36.4 %collective-permute-start.31 = (bf16[2,128,1536]{2,1,0:T(8,128)(2,1)S(1)}, bf16[2,128,1536]{2,1,0:T(8,128)(2,1)S(1)}, u32[]{:S(2)}, u32[]{:S(2)}) collective-permute-start(bf16[2,128,1536]{2,1,0:T(8,128)(2,1)S(1)} %pad_maximum_fusion.8), channel_id=1, source_target_pairs={{0,24},{8,0},{16,8},{24,16},{1,25},{9,1},{17,9},{25,17},{2,26},{10... | collective-permute-start | bytes 2359304 | tf_op jit(solution)/shard_map/ppermute | solution.py:43
  143.3 23.5 %collective-permute-start.14 = (bf16[128,1536]{1,0:T(8,128)(2,1)S(1)}, bf16[128,1536]{1,0:T(8,128)(2,1)S(1)}, u32[]{:S(2)}, u32[]{:S(2)}) collective-permute-start(bf16[128,1536]{1,0:T(8,128)(2,1)S(1)} %slice_bitcast_fusion.6), channel_id=1, source_target_pairs={{0,8},{8,16},{16,24},{24,0},{1,9},{9,17},{17,25},{25,1},{2,10},{10... | collective-permute-start | bytes 1179656 | tf_op jit(solution)/shard_map/ppermute | solution.py:43
  143.4 23.3 %collective-permute-start.12 = (bf16[128,1536]{1,0:T(8,128)(2,1)S(1)}, bf16[128,1536]{1,0:T(8,128)(2,1)S(1)}, u32[]{:S(2)}, u32[]{:S(2)}) collective-permute-start(bf16[128,1536]{1,0:T(8,128)(2,1)S(1)} %slice_bitcast_fusion.7), channel_id=1, source_target_pairs={{0,24},{8,0},{16,8},{24,16},{1,25},{9,1},{17,9},{25,17},{2,26},{10... | collective-permute-start | bytes 1179656 | tf_op jit(solution)/shard_map/ppermute | solution.py:43
  160.1 13.1 %collective-permute-start.34 = (bf16[128,1536]{1,0:T(8,128)(2,1)S(1)}, bf16[128,1536]{1,0:T(8,128)(2,1)S(1)}, u32[]{:S(2)}, u32[]{:S(2)}) collective-permute-start(bf16[128,1536]{1,0:T(8,128)(2,1)S(1)} %slice_bitcast_fusion.2), channel_id=1, source_target_pairs={{0,8},{8,16},{16,24},{24,0},{1,9},{9,17},{17,25},{25,1},{2,10},{10... | collective-permute-start | bytes 1179656 | tf_op jit(solution)/shard_map/ppermute | solution.py:43
  162.6 10.6 %collective-permute-start.32 = (bf16[128,1536]{1,0:T(8,128)(2,1)S(1)}, bf16[128,1536]{1,0:T(8,128)(2,1)S(1)}, u32[]{:S(2)}, u32[]{:S(2)}) collective-permute-start(bf16[128,1536]{1,0:T(8,128)(2,1)S(1)} %slice_bitcast_fusion.3), channel_id=1, source_target_pairs={{0,24},{8,0},{16,8},{24,16},{1,25},{9,1},{17,9},{25,17},{2,26},{10... | collective-permute-start | bytes 1179656 | tf_op jit(solution)/shard_map/ppermute | solution.py:43
  167.9 11.7 %collective-permute-start.15 = (bf16[4,2,8,8,768]{4,3,2,1,0:T(8,128)(2,1)S(1)}, bf16[4,2,8,8,768]{4,3,2,1,0:T(8,128)(2,1)S(1)}, u32[]{:S(2)}, u32[]{:S(2)}) collective-permute-start(bf16[4,2,8,8,768]{4,3,2,1,0:T(8,128)(2,1)S(1)} %slice.225), channel_id=1, source_target_pairs={{0,32},{32,0},{1,33},{33,1},{2,34},{34,2},{3,35},{35,3},{4,36},{36... | collective-permute-start | bytes 2359304 | tf_op jit(solution)/shard_map/ppermute | solution.py:43
  179.9 12.7 %collective-permute-start.16 = (bf16[4,2,2,8,768]{4,3,2,1,0:T(8,128)(2,1)S(1)}, bf16[4,2,2,8,768]{4,3,2,1,0:T(8,128)(2,1)S(1)}, u32[]{:S(2)}, u32[]{:S(2)}) collective-permute-start(bf16[4,2,2,8,768]{4,3,2,1,0:T(8,128)(2,1)S(1)} %get-tuple-element.23), channel_id=1, source_target_pairs={{0,1},{1,2},{2,3},{3,0},{4,5},{5,6},{6,7},{7,4},{8,9},{9,10},{10,1... | collective-permute-start | bytes 589832 | tf_op jit(solution)/shard_map/ppermute | solution.py:43
  180.0 12.6 %collective-permute-start.18 = (bf16[4,2,2,8,768]{4,3,2,1,0:T(8,128)(2,1)S(1)}, bf16[4,2,2,8,768]{4,3,2,1,0:T(8,128)(2,1)S(1)}, u32[]{:S(2)}, u32[]{:S(2)}) collective-permute-start(bf16[4,2,2,8,768]{4,3,2,1,0:T(8,128)(2,1)S(1)} %get-tuple-element.24), channel_id=1, source_target_pairs={{0,3},{1,0},{2,1},{3,2},{4,7},{5,4},{6,5},{7,6},{8,11},{9,8},{10,9... | collective-permute-start | bytes 589832 | tf_op jit(solution)/shard_map/ppermute | solution.py:43
  184.1 16.0 %collective-permute-start.36 = (bf16[4,2,2,8,768]{4,3,2,1,0:T(8,128)(2,1)S(1)}, bf16[4,2,2,8,768]{4,3,2,1,0:T(8,128)(2,1)S(1)}, u32[]{:S(2)}, u32[]{:S(2)}) collective-permute-start(bf16[4,2,2,8,768]{4,3,2,1,0:T(8,128)(2,1)S(1)} %get-tuple-element.18), channel_id=1, source_target_pairs={{0,1},{1,2},{2,3},{3,0},{4,5},{5,6},{6,7},{7,4},{8,9},{9,10},{10,1... | collective-permute-start | bytes 589832 | tf_op jit(solution)/shard_map/ppermute | solution.py:43
  184.4 15.7 %collective-permute-start.38 = (bf16[4,2,2,8,768]{4,3,2,1,0:T(8,128)(2,1)S(1)}, bf16[4,2,2,8,768]{4,3,2,1,0:T(8,128)(2,1)S(1)}, u32[]{:S(2)}, u32[]{:S(2)}) collective-permute-start(bf16[4,2,2,8,768]{4,3,2,1,0:T(8,128)(2,1)S(1)} %get-tuple-element.19), channel_id=1, source_target_pairs={{0,3},{1,0},{2,1},{3,2},{4,7},{5,4},{6,5},{7,6},{8,11},{9,8},{10,9... | collective-permute-start | bytes 589832 | tf_op jit(solution)/shard_map/ppermute | solution.py:43
  192.8 10.0 %collective-permute-start.19 = (bf16[4,2,8,768]{3,2,1,0:T(8,128)(2,1)S(1)}, bf16[4,2,8,768]{3,2,1,0:T(8,128)(2,1)S(1)}, u32[]{:S(2)}, u32[]{:S(2)}) collective-permute-start(bf16[4,2,8,768]{3,2,1,0:T(8,128)(2,1)S(1)} %slice_bitcast_fusion.12), channel_id=1, source_target_pairs={{0,64},{64,0},{1,65},{65,1},{2,66},{66,2},{3,67},{67,3},{4,68},{68... | collective-permute-start | bytes 294920 | tf_op jit(solution)/shard_map/ppermute | solution.py:43
  (16 other events, 126.9 us)

commit v3 on v2

v3 whole, which is shorter than its diff:
```python
import functools
import math

import jax
import jax.numpy as jnp
from jax import lax
from jax.experimental import pallas as pl
from jax.experimental.pallas import tpu as pltpu
from jax.sharding import Mesh
from jax.sharding import PartitionSpec as P

tanh_scale = math.sqrt(2.0 / math.pi)
cubic_coef = 0.044715
AXES = ("xl", "c", "z", "xh", "y")


def gelu_parts(preact):
    inner = tanh_scale * (preact + cubic_coef * preact * preact * preact)
    hyper = jnp.tanh(inner)
    activated = 0.5 * preact * (1.0 + hyper)
    derivative = 0.5 * (1.0 + hyper) + 0.5 * preact * (1.0 - hyper * hyper) * tanh_scale * (
        1.0 + 3.0 * cubic_coef * preact * preact
    )
    return (activated, derivative)


def contract(left, right, left_dim, right_dim):
    return lax.dot_general(
        left,
        right,
        (((left_dim,), (right_dim,)), ((), ())),
        preferred_element_type=jnp.float32,
    )


def product_kernel(dim, *refs):
    count = (len(refs) - 1) // 2
    right = refs[count][...]
    for left_ref, out_ref in zip(refs[:count], refs[count + 1 :], strict=True):
        out_ref[...] = lax.dot_general(
            left_ref[...], right, (((1,), (dim,)), ((), ())), preferred_element_type=jnp.float32
        ).astype(out_ref.dtype)


def products(lefts, right, dim):
    rows, depth = lefts[0].shape
    total = right.shape[1 - dim]
    width = total // 3
    shape = (depth, width) if dim == 0 else (width, depth)
    return pl.pallas_call(
        functools.partial(product_kernel, dim),
        grid=(3,),
        out_shape=[jax.ShapeDtypeStruct((rows, total), jnp.bfloat16) for _ in lefts],
        in_specs=[pl.BlockSpec((rows, depth), lambda i: (0, 0)) for _ in lefts]
        + [pl.BlockSpec(shape, (lambda i: (0, i)) if dim == 0 else (lambda i: (i, 0)))],
        out_specs=[pl.BlockSpec((rows, width), lambda i: (0, i)) for _ in lefts],
        compiler_params=pltpu.CompilerParams(vmem_limit_bytes=32 * 2**20),
        cost_estimate=pl.CostEstimate(flops=1024, bytes_accessed=1024, transcendentals=0),
    )(*lefts, right)


def low(value):
    return value.astype(jnp.bfloat16)


def wide(value):
    return value.astype(jnp.float32)


def send(value, axis, step):
    count = lax.axis_size(axis)
    return lax.ppermute(value, axis, [(i, (i + step) % count) for i in range(count)])


def relative(value):
    value = value.reshape(4, 2, 8, value.shape[-1])
    value = lax.dynamic_slice_in_dim(jnp.concatenate([value, value], 0), lax.axis_index("z"), 4, 0)
    return lax.dynamic_slice_in_dim(jnp.concatenate([value, value], 1), lax.axis_index("xh"), 2, 1)


def absolute(value):
    width = value.shape[-1]
    value = lax.dynamic_slice_in_dim(
        jnp.concatenate([value, value], 1), (2 - lax.axis_index("xh")) % 2, 2, 1
    )
    value = lax.dynamic_slice_in_dim(
        jnp.concatenate([value, value], 0), (4 - lax.axis_index("z")) % 4, 4, 0
    )
    return value.reshape(64, width)


def after(kept, value, *others):
    value, others = lax.optimization_barrier((value, others))
    kept.extend(jax.tree.leaves(others))
    return value


def outer_kernel(count, scale, *refs):
    total = 0.0
    for left_ref, right_ref in zip(refs[:count], refs[count : 2 * count], strict=True):
        total = total + lax.dot_general(
            left_ref[...],
            right_ref[...],
            (((0,), (0,)), ((), ())),
            preferred_element_type=jnp.float32,
        )
    refs[-1][...] = (total * scale).astype(jnp.bfloat16)


def outer(lefts, rights, scale, kept=()):
    depth, rows = lefts[0].shape
    total = rights[0].shape[1]
    if rows > total:
        block = rows // 3
        left_spec = pl.BlockSpec((depth, block), lambda i: (0, i))
        right_spec = pl.BlockSpec((depth, total), lambda i: (0, 0))
        out_spec = pl.BlockSpec((block, total), lambda i: (i, 0))
    else:
        block = total // 3
        left_spec = pl.BlockSpec((depth, rows), lambda i: (0, 0))
        right_spec = pl.BlockSpec((depth, block), lambda i: (0, i))
        out_spec = pl.BlockSpec((rows, block), lambda i: (0, i))
    return pl.pallas_call(
        functools.partial(outer_kernel, len(lefts), scale),
        grid=(3,),
        out_shape=jax.ShapeDtypeStruct((rows, total), jnp.bfloat16),
        in_specs=[left_spec] * len(lefts)
        + [right_spec] * len(rights)
        + [pl.BlockSpec(memory_space=pl.ANY)] * len(kept),
        out_specs=out_spec,
        compiler_params=pltpu.CompilerParams(vmem_limit_bytes=48 * 2**20),
        cost_estimate=pl.CostEstimate(flops=1024, bytes_accessed=1024, transcendentals=0),
    )(*lefts, *rights, *kept)


def together(*values):
    return lax.optimization_barrier(values)


def gather_x(value):
    value = value[:, :, None]
    return jnp.concatenate([value, send(value, "xl", 1)], 2)


def gather_y(value):
    return [value] + [send(value, "y", -d) for d in (1, 2, 3)]


def send_blocks(value, axis, step):
    return jnp.concatenate([send(value[i : i + 1], axis, step) for i in range(value.shape[0])])


def gather_c(parts):
    value = jnp.concatenate(parts, 2)
    return [
        jnp.concatenate([block, send(block, "c", 1)], 1).reshape(256, block.shape[-1])
        for block in value
    ]


def scatter_c(value):
    return low(wide(value[:, :, :8]) + wide(send_blocks(value[:, :, 8:], "c", 1)))


def scatter_y(value):
    return [value[:, :, :2]] + [send(value[:, :, 2 * d : 2 * d + 2], "y", d) for d in (1, 2, 3)]


def scatter_x(parts):
    value = low(sum(wide(part) for part in parts))
    return value[:, :, 0], send(value[:, :, 1], "xl", 1)


def wid_first(block):
    return send(block[0], "z", 1), send(block[1], "z", -1)


def wid_second_terms(blocks, first):
    to_next = blocks[1].at[0].set(low(wide(blocks[1][0]) + wide(first[0])))
    to_last = blocks[3].at[1].set(low(wide(blocks[3][1]) + wide(first[1])))
    return to_next, to_last


def wid_second(pair):
    return send(pair[0], "z", 1), send(pair[1], "z", -1)


def wid_third(blocks, second):
    parts = [blocks[0], *second]
    other = low(sum(wide(part[1]) for part in parts))
    return sum(wide(part[0]) for part in parts), other


def local(tokens, up_weight, down_weight, cotangent):
    width = tokens.shape[-1]
    hidden = up_weight.shape[-1]
    grad_scale = 1.0 / math.sqrt(1024.0)

    def terms(lefts, right, dim):
        return [r.reshape(2, 128, hidden) for r in products(lefts, right, dim)]

    def out_terms(parts, right, dim):
        parts = [p.reshape(256, hidden) for p in parts]
        return jnp.stack(products(parts, right, dim)).reshape(-1, 2, 16, 8, width)

    kept = []
    wait = functools.partial(after, kept)
    tok_rel = relative(tokens)
    far_x = gather_x(tok_rel[2:3])
    far_y = gather_y(far_x)
    rest_x = gather_x(jnp.stack([tok_rel[0], tok_rel[1], tok_rel[3]]))
    cot_x = gather_x(relative(cotangent))
    rest_y = gather_y(wait(rest_x, far_y))
    tok_far = gather_c(far_y)
    pre_far = terms([tok_far[0]], up_weight, 0)[0]
    pre_first = wid_first(pre_far)
    tok_rest = gather_c(wait(rest_y, pre_far))
    pre_own, pre_next, pre_last = terms(list(tok_rest), up_weight, 0)
    pre = [pre_own, pre_next, pre_far, pre_last]
    cot_y = gather_y(wait(cot_x, pre_own))
    pre_pair = wid_second_terms(pre, pre_first)
    pre_second = wid_second(pre_pair)
    cot_all = gather_c(wait(cot_y, pre_pair))
    grad = terms(list(cot_all), down_weight, 1)
    grad_first = wid_first(grad[2])
    pre_here, pre_other = wid_third(pre, pre_second)
    grad_first = wait(grad_first, pre_other)
    grad_pair = wid_second_terms(grad, grad_first)
    grad_second = wid_second(grad_pair)
    pre_there = send(pre_other, "xh", 1)
    activated, derivative = gelu_parts(pre_here + wide(pre_there))
    act_here = low(activated)
    act_there = send(act_here, "xh", 1)
    act_here_near = together(send(act_here, "z", -1), send(act_here, "z", 1))
    grad_second = wait(grad_second, act_there)
    act_there_near = together(send(act_there, "z", -1), send(act_there, "z", 1))
    grad_here, grad_other = wid_third(grad, grad_second)
    grad_there = send(grad_other, "xh", 1)
    act_far_here = send(act_here_near[0], "z", -1)
    hgrad_here = low((grad_here + wide(grad_there)) * derivative)
    hgrad_there = send(hgrad_here, "xh", 1)
    hgrad_here_near = together(send(hgrad_here, "z", -1), send(hgrad_here, "z", 1))
    act_there_near = wait(act_there_near, hgrad_here)
    act_far_there = send(act_there_near[1], "z", 1)
    act_far_there = wait(act_far_there, hgrad_there)
    act = [
        jnp.stack(pair)
        for pair in (
            (act_here, act_there),
            (act_here_near[0], act_there_near[0]),
            (act_far_here, act_far_there),
            (act_here_near[1], act_there_near[1]),
        )
    ]
    hgrad_there_near = together(send(hgrad_there, "z", -1), send(hgrad_there, "z", 1))
    out_c = scatter_c(out_terms(act, down_weight, 0))
    out_y = scatter_y(out_c)
    hgrad_far_here = send(hgrad_here_near[0], "z", -1)
    hgrad_far_there = send(hgrad_there_near[1], "z", 1)
    act_parts = wait([part.reshape(256, hidden) for part in act], out_c)
    down_grad = outer(act_parts, list(cot_all), grad_scale)
    out_y = wait(out_y, hgrad_far_here, hgrad_there_near, down_grad)
    hgrad = [
        jnp.stack(pair)
        for pair in (
            (hgrad_here, hgrad_there),
            (hgrad_here_near[0], hgrad_there_near[0]),
            (hgrad_far_here, hgrad_far_there),
            (hgrad_here_near[1], hgrad_there_near[1]),
        )
    ]
    near_c = scatter_c(out_terms([hgrad[0], hgrad[1], hgrad[3]], up_weight, 1))
    out_parts = scatter_x(out_y)
    near_y = scatter_y(near_c)
    hgrad_far = wait(hgrad[2], near_y)
    far_c = scatter_c(out_terms([hgrad_far], up_weight, 1))
    far_y = scatter_y(far_c)
    hgrad_parts = wait([part.reshape(256, hidden) for part in hgrad], far_c)
    tok_parts = [tok_rest[0], tok_rest[1], tok_far[0], tok_rest[2]]
    up_grad = outer(tok_parts, hgrad_parts, grad_scale, kept)
    back_parts = scatter_x(
        [jnp.concatenate([n[:2], f, n[2:]]) for n, f in zip(near_y, far_y, strict=True)]
    )
    layer_out = low(wide(out_parts[0]) + wide(out_parts[1]))
    tokens_grad = low(wide(back_parts[0]) + wide(back_parts[1]))
    return (absolute(layer_out), absolute(tokens_grad), up_grad, down_grad)


def solution(mesh):
    fine = Mesh(mesh.devices.reshape(2, 2, 4, 2, 4), AXES)
    rows = P(("xl", "c", "y"), ("z", "xh"))
    up_spec = P(("z", "xh"), ("y", "xl", "c"))
    down_spec = P(("y", "xl", "c"), ("z", "xh"))
    return jax.shard_map(
        local,
        mesh=fine,
        in_specs=(rows, up_spec, down_spec, rows),
        out_specs=(rows, rows, up_spec, down_spec),
        check_vma=False,
    )
```

time: 208 us -> 193 us (0.928)
  waiting for transfers between devices: 110 us -> 73.4 us
  Pallas kernels: 0 us -> 24.1 us
  matrix products: 20.5 us -> 0 us
  starting transfers between devices: 60.7 us -> 78.2 us
  other arithmetic: 8.03 us -> 13.2 us
  local copies, waits for them, and re-layouts: 6.6 us -> 1.45 us
    ppermute x40 -> x63, waiting for transfers between devices: 110 us -> 73.4 us  [send(): lax.ppermute(value, axis, [(i, (i + step) % count) for i in range(count)])]
    pallas_call x0 -> x8, Pallas kernels: none -> 24.1 us  [the longest x6 14.3 us: products(): pl.pallas_call(functools.partial(product_kernel, dim), grid=(3,), out_sha...]
    dot_general x18 -> x0, matrix products: 20.5 us -> none  [contract(): lax.dot_general(left, right, (((left_dim,), (right_dim,)), ((), ())), pre...]
    ppermute x40 -> x63, starting transfers between devices: 60.7 us -> 78.2 us  [send(): lax.ppermute(value, axis, [(i, (i + step) % count) for i in range(count)])]
    unnamed x24 -> x100, local copies, waits for them, and re-layouts: 5.6 us -> 0.79 us
    convert_element_type x7 -> x11, other arithmetic: 1.31 us -> 5.66 us  [low(): return value.astype(jnp.bfloat16)]
  transfers between devices with their start and end apart: 40 -> 63, of which waited for: 20 -> 32; matrix products, arithmetic and copies ran while one was open for 13% -> 6% of each run, Pallas kernels for 0% -> 13%
where the time goes in v3:
time: 193 us; the launch traced here: 192 us
  starting transfers between devices  78.2 us (41%)
  waiting for transfers between devices  73.4 us (38%)
  Pallas kernels  24.1 us (12%)
  other arithmetic  13.2 us (7%)
    ppermute x63, starting transfers between devices, send(): lax.ppermute(value, axis, [(i, (i + step) % count) for i in range(count)])  78.2 us
    ppermute x63, waiting for transfers between devices, send(): lax.ppermute(value, axis, [(i, (i + step) % count) for i in range(count)])  73.4 us
    pallas_call x6, Pallas kernels, products(): pl.pallas_call(functools.partial(product_kernel, dim), grid=(3,), out_sha...  14.3 us
    pallas_call x2, Pallas kernels, outer(): pl.pallas_call(functools.partial(outer_kernel, len(lefts), scale), grid=(...  9.75 us
    convert_element_type x11, other arithmetic, low(): return value.astype(jnp.bfloat16)  5.66 us
  transfers between devices with their start and end apart: 63, of which 32 were waited for; matrix products, arithmetic and copies ran while one was open for 6% of the time, Pallas kernels for 13%

profile of v3, /device:TPU:0, one launch (start us, length us, event | category | flops | bytes accessed | tf_op | source)
XLA Modules:
  0.0 192.2 jit_solution(17456788597453125715)
XLA Ops:
  7.6 2.9 %collective-permute-start.3 = (bf16[1,2,2,8,768]{4,3,2,1,0:T(8,128)(2,1)S(1)}, bf16[1,2,2,8,768]{4,3,2,1,0:T(8,128)(2,1)S(1)}, u32[]{:S(2)}, u32[]{:S(2)}) collective-permute-start(bf16[1,2,2,8,768]{4,3,2,1,0:T(8,128)(2,1)S(1)} %pad_maximum_fusion.23.refs_8_), channel_id=1, source_target_pairs={{0,2},{1,3},{2,0},{3,1},{4,6},{5,7},{6,4},{7,5},{8,10},{9,11},{10,... | collective-permute-start | bytes 147464 | tf_op jit(solution)/shard_map/ppermute | solution.py:72
  11.8 2.7 %collective-permute-done.2.refs_9_ = bf16[1,2,2,8,768]{4,3,2,1,0:T(8,128)(2,1)S(1)} collective-permute-done((bf16[1,2,2,8,768]{4,3,2,1,0:T(8,128)(2,1)S(1)}, bf16[1,2,2,8,768]{4,3,2,1,0:T(8,128)(2,1)S(1)}, u32[]{:S(2)}, u32[]{:S(2)}) %collective-permute-start.2) | collective-permute-done | bytes 49184 | tf_op jit(solution)/shard_map/ppermute | solution.py:72
  15.0 3.9 %collective-permute-start.6 = (bf16[3,2,2,8,768]{4,3,1,0,2:T(8,128)(2,1)S(1)}, bf16[3,2,2,8,768]{4,3,1,0,2:T(8,128)(2,1)S(1)}, u32[]{:S(2)}, u32[]{:S(2)}) collective-permute-start(bf16[3,2,2,8,768]{4,3,1,0,2:T(8,128)(2,1)S(1)} %pad_maximum_fusion.22), channel_id=1, source_target_pairs={{0,2},{1,3},{2,0},{3,1},{4,6},{5,7},{6,4},{7,5},{8,10},{9,11},{10,... | collective-permute-start | bytes 442376 | tf_op jit(solution)/shard_map/ppermute | solution.py:72
  22.3 3.9 %collective-permute-done.6 = bf16[3,2,2,8,768]{4,3,1,0,2:T(8,128)(2,1)S(1)} collective-permute-done((bf16[3,2,2,8,768]{4,3,1,0,2:T(8,128)(2,1)S(1)}, bf16[3,2,2,8,768]{4,3,1,0,2:T(8,128)(2,1)S(1)}, u32[]{:S(2)}, u32[]{:S(2)}) %collective-permute-start.6) | collective-permute-done | bytes 147488 | tf_op jit(solution)/shard_map/ppermute | solution.py:72
  27.1 4.0 %collective-permute-start.14 = (bf16[128,1536]{1,0:T(8,128)(2,1)S(1)}, bf16[128,1536]{1,0:T(8,128)(2,1)S(1)}, u32[]{:S(2)}, u32[]{:S(2)}) collective-permute-start(bf16[128,1536]{1,0:T(8,128)(2,1)S(1)} %get-tuple-element.211), channel_id=1, source_target_pairs={{0,24},{8,0},{16,8},{24,16},{1,25},{9,1},{17,9},{25,17},{2,26},{10... | collective-permute-start | bytes 1179656 | tf_op jit(solution)/shard_map/ppermute | solution.py:72
  32.8 2.7 %shard_map.76 = (bf16[256,1536]{1,0:T(8,128)(2,1)S(1)}, bf16[256,1536]{1,0:T(8,128)(2,1)S(1)}, bf16[256,1536]{1,0:T(8,128)(2,1)S(1)}) custom-call(bf16[256,768]{1,0:T(8,128)(2,1)S(1)} %bitcast.172, bf16[256,768]{1,0:T(8,128)(2,1)S(1)} %bitcast.170, bf16[256,768]{1,0:T(8,128)(2,1)S(1)} %bitcast.168, bf16[768,1536]{1,0:T(8,128)(2,1)S(1)} %copy-done), custom_call_target="tpu_custom_call" | custom-call | flops 1024 | bytes 1024 | tf_op jit(solution)/shard_map/pallas_call | solution.py:50
  36.2 3.3 %collective-permute-start.24 = (bf16[4,2,2,8,768]{4,3,2,1,0:T(8,128)(2,1)S(1)}, bf16[4,2,2,8,768]{4,3,2,1,0:T(8,128)(2,1)S(1)}, u32[]{:S(2)}, u32[]{:S(2)}) collective-permute-start(bf16[4,2,2,8,768]{4,3,2,1,0:T(8,128)(2,1)S(1)} %pad_maximum_fusion.21), channel_id=1, source_target_pairs={{0,2},{1,3},{2,0},{3,1},{4,6},{5,7},{6,4},{7,5},{8,10},{9,11},{10,... | collective-permute-start | bytes 589832 | tf_op jit(solution)/shard_map/ppermute | solution.py:72
  39.8 4.1 %collective-permute-done.12 = bf16[128,1536]{1,0:T(8,128)(2,1)S(1)} collective-permute-done((bf16[128,1536]{1,0:T(8,128)(2,1)S(1)}, bf16[128,1536]{1,0:T(8,128)(2,1)S(1)}, u32[]{:S(2)}, u32[]{:S(2)}) %collective-permute-start.12) | collective-permute-done | bytes 393248 | tf_op jit(solution)/shard_map/ppermute | solution.py:72
  44.1 4.5 %collective-permute-done.24 = bf16[4,2,2,8,768]{4,3,2,1,0:T(8,128)(2,1)S(1)} collective-permute-done((bf16[4,2,2,8,768]{4,3,2,1,0:T(8,128)(2,1)S(1)}, bf16[4,2,2,8,768]{4,3,2,1,0:T(8,128)(2,1)S(1)}, u32[]{:S(2)}, u32[]{:S(2)}) %collective-permute-start.24) | collective-permute-done | bytes 196640 | tf_op jit(solution)/shard_map/ppermute | solution.py:72
  49.4 3.2 %collective-permute-start.15 = (bf16[2,128,1536]{2,1,0:T(8,128)(2,1)S(1)}, bf16[2,128,1536]{2,1,0:T(8,128)(2,1)S(1)}, u32[]{:S(2)}, u32[]{:S(2)}) collective-permute-start(bf16[2,128,1536]{2,1,0:T(8,128)(2,1)S(1)} %fusion.14.refs_15_), channel_id=1, source_target_pairs={{0,24},{8,0},{16,8},{24,16},{1,25},{9,1},{17,9},{25,17},{2,26},{10... | collective-permute-start | bytes 2359304 | tf_op jit(solution)/shard_map/ppermute | solution.py:72
  54.5 3.2 %shard_map.77 = (bf16[256,1536]{1,0:T(8,128)(2,1)S(1)}, bf16[256,1536]{1,0:T(8,128)(2,1)S(1)}, bf16[256,1536]{1,0:T(8,128)(2,1)S(1)}, bf16[256,1536]{1,0:T(8,128)(2,1)S(1)}) custom-call(bf16[256,768]{1,0:T(8,128)(2,1)S(1)} %bitcast.181, bf16[256,768]{1,0:T(8,128)(2,1)S(1)} %bitcast.179, bf16[256,768]{1,0:T(8,128)(2,1)S(1)} %bitcast.177, ...), custom_call_target="tpu_custom_call" | custom-call | flops 1024 | bytes 1024 | tf_op jit(solution)/shard_map/pallas_call | solution.py:50
  60.1 10.8 %collective-permute-done.13 = bf16[2,128,1536]{2,1,0:T(8,128)(2,1)S(1)} collective-permute-done((bf16[2,128,1536]{2,1,0:T(8,128)(2,1)S(1)}, bf16[2,128,1536]{2,1,0:T(8,128)(2,1)S(1)}, u32[]{:S(2)}, u32[]{:S(2)}) %collective-permute-start.13) | collective-permute-done | bytes 786464 | tf_op jit(solution)/shard_map/ppermute | solution.py:72
  71.1 3.3 %collective-permute-start.16 = (bf16[128,1536]{1,0:T(8,128)(2,1)S(1)}, bf16[128,1536]{1,0:T(8,128)(2,1)S(1)}, u32[]{:S(2)}, u32[]{:S(2)}) collective-permute-start(bf16[128,1536]{1,0:T(8,128)(2,1)S(1)} %fusion.9.refs_16_), channel_id=1, source_target_pairs={{0,4},{4,0},{1,5},{5,1},{2,6},{6,2},{3,7},{7,3},{8,12},{12,8},{9,1... | collective-permute-start | bytes 1179656 | tf_op jit(solution)/shard_map/ppermute | solution.py:72
  74.4 3.4 %collective-permute-done.31 = bf16[128,1536]{1,0:T(8,128)(2,1)S(1)} collective-permute-done((bf16[128,1536]{1,0:T(8,128)(2,1)S(1)}, bf16[128,1536]{1,0:T(8,128)(2,1)S(1)}, u32[]{:S(2)}, u32[]{:S(2)}) %collective-permute-start.31) | collective-permute-done | bytes 393248 | tf_op jit(solution)/shard_map/ppermute | solution.py:72
  83.3 3.2 %collective-permute-start.17 = (bf16[128,1536]{1,0:T(8,128)(2,1)}, bf16[128,1536]{1,0:T(8,128)(2,1)}, u32[]{:S(2)}, u32[]{:S(2)}) collective-permute-start(bf16[128,1536]{1,0:T(8,128)(2,1)} %multiply_convert_fusion), channel_id=1, source_target_pairs={{0,4},{4,0},{1,5},{5,1},{2,6},{6,2},{3,7},{7,3},{8,12},{12,8},{9,1... | collective-permute-start | bytes 1179656 | tf_op jit(solution)/shard_map/ppermute | solution.py:72
  89.8 5.1 %collective-permute-done.17.refs_17_ = bf16[128,1536]{1,0:T(8,128)(2,1)} collective-permute-done((bf16[128,1536]{1,0:T(8,128)(2,1)}, bf16[128,1536]{1,0:T(8,128)(2,1)}, u32[]{:S(2)}, u32[]{:S(2)}) %collective-permute-start.17) | collective-permute-done | bytes 393248 | tf_op jit(solution)/shard_map/ppermute | solution.py:72
  94.9 5.5 %collective-permute-done.32 = bf16[2,128,1536]{2,1,0:T(8,128)(2,1)S(1)} collective-permute-done((bf16[2,128,1536]{2,1,0:T(8,128)(2,1)S(1)}, bf16[2,128,1536]{2,1,0:T(8,128)(2,1)S(1)}, u32[]{:S(2)}, u32[]{:S(2)}) %collective-permute-start.32) | collective-permute-done | bytes 786464 | tf_op jit(solution)/shard_map/ppermute | solution.py:72
  101.6 3.2 %collective-permute-start.34 = (bf16[128,1536]{1,0:T(8,128)(2,1)}, bf16[128,1536]{1,0:T(8,128)(2,1)}, u32[]{:S(2)}, u32[]{:S(2)}) collective-permute-start(bf16[128,1536]{1,0:T(8,128)(2,1)} %fusion.7), channel_id=1, source_target_pairs={{0,4},{4,0},{1,5},{5,1},{2,6},{6,2},{3,7},{7,3},{8,12},{12,8},{9,1... | collective-permute-start | bytes 1179656 | tf_op jit(solution)/shard_map/ppermute | solution.py:72
  107.1 3.1 %collective-permute-start.35 = (bf16[128,1536]{1,0:T(8,128)(2,1)}, bf16[128,1536]{1,0:T(8,128)(2,1)S(1)}, u32[]{:S(2)}, u32[]{:S(2)}) collective-permute-start(bf16[128,1536]{1,0:T(8,128)(2,1)} %collective-permute-done.18), channel_id=1, source_target_pairs={{0,24},{8,0},{16,8},{24,16},{1,25},{9,1},{17,9},{25,17},{2,26},{10... | collective-permute-start | bytes 1179656 | tf_op jit(solution)/shard_map/ppermute | solution.py:72
  110.3 3.2 %collective-permute-start.20 = (bf16[128,1536]{1,0:T(8,128)(2,1)}, bf16[128,1536]{1,0:T(8,128)(2,1)S(1)}, u32[]{:S(2)}, u32[]{:S(2)}) collective-permute-start(bf16[128,1536]{1,0:T(8,128)(2,1)} %collective-permute-done.17.refs_17_), channel_id=1, source_target_pairs={{0,24},{8,0},{16,8},{24,16},{1,25},{9,1},{17,9},{25,17},{2,26},{10... | collective-permute-start | bytes 1179656 | tf_op jit(solution)/shard_map/ppermute | solution.py:72
  117.1 3.2 %collective-permute-start.45 = (bf16[128,1536]{1,0:T(8,128)(2,1)S(1)}, bf16[128,1536]{1,0:T(8,128)(2,1)S(1)}, u32[]{:S(2)}, u32[]{:S(2)}) collective-permute-start(bf16[128,1536]{1,0:T(8,128)(2,1)S(1)} %fusion.6.refs_18_), channel_id=1, source_target_pairs={{0,24},{8,0},{16,8},{24,16},{1,25},{9,1},{17,9},{25,17},{2,26},{10... | collective-permute-start | bytes 1179656 | tf_op jit(solution)/shard_map/ppermute | solution.py:72
  122.7 3.2 %collective-permute-start.37 = (bf16[128,1536]{1,0:T(8,128)(2,1)S(1)}, bf16[128,1536]{1,0:T(8,128)(2,1)S(1)}, u32[]{:S(2)}, u32[]{:S(2)}) collective-permute-start(bf16[128,1536]{1,0:T(8,128)(2,1)S(1)} %fusion.6.refs_18_), channel_id=1, source_target_pairs={{0,4},{4,0},{1,5},{5,1},{2,6},{6,2},{3,7},{7,3},{8,12},{12,8},{9,1... | collective-permute-start | bytes 1179656 | tf_op jit(solution)/shard_map/ppermute | solution.py:72
  125.9 2.6 %collective-permute-done.20 = bf16[128,1536]{1,0:T(8,128)(2,1)S(1)} collective-permute-done((bf16[128,1536]{1,0:T(8,128)(2,1)}, bf16[128,1536]{1,0:T(8,128)(2,1)S(1)}, u32[]{:S(2)}, u32[]{:S(2)}) %collective-permute-start.20) | collective-permute-done | bytes 393248 | tf_op jit(solution)/shard_map/ppermute | solution.py:72
  131.1 2.8 %collective-permute-done.45 = bf16[128,1536]{1,0:T(8,128)(2,1)S(1)} collective-permute-done((bf16[128,1536]{1,0:T(8,128)(2,1)S(1)}, bf16[128,1536]{1,0:T(8,128)(2,1)S(1)}, u32[]{:S(2)}, u32[]{:S(2)}) %collective-permute-start.45) | collective-permute-done | bytes 393248 | tf_op jit(solution)/shard_map/ppermute | solution.py:72
  133.9 3.7 %collective-permute-start.47 = (bf16[128,1536]{1,0:T(8,128)(2,1)S(1)}, bf16[128,1536]{1,0:T(8,128)(2,1)S(1)}, u32[]{:S(2)}, u32[]{:S(2)}) collective-permute-start(bf16[128,1536]{1,0:T(8,128)(2,1)S(1)} %collective-permute-done.45), channel_id=1, source_target_pairs={{0,24},{8,0},{16,8},{24,16},{1,25},{9,1},{17,9},{25,17},{2,26},{10... | collective-permute-start | bytes 1179656 | tf_op jit(solution)/shard_map/ppermute | solution.py:72
  138.0 3.2 %shard_map.78 = (bf16[256,768]{1,0:T(8,128)(2,1)S(1)}, bf16[256,768]{1,0:T(8,128)(2,1)S(1)}, bf16[256,768]{1,0:T(8,128)(2,1)S(1)}, bf16[256,768]{1,0:T(8,128)(2,1)S(1)}) custom-call(bf16[256,1536]{1,0:T(8,128)(2,1)S(1)} %bitcast.157, bf16[256,1536]{1,0:T(8,128)(2,1)S(1)} %bitcast.159, bf16[256,1536]{1,0:T(8,128)(2,1)S(1)} %bitcast.163, ...), custom_call_target="tpu_custom_call" | custom-call | flops 1024 | bytes 1024 | tf_op jit(solution)/shard_map/pallas_call | solution.py:50
  143.2 3.0 %collective-permute-start.48 = (bf16[128,1536]{1,0:T(8,128)(2,1)S(1)}, bf16[128,1536]{1,0:T(8,128)(2,1)S(1)}, u32[]{:S(2)}, u32[]{:S(2)}) collective-permute-start(bf16[128,1536]{1,0:T(8,128)(2,1)S(1)} %collective-permute-done.37.refs_19_), channel_id=1, source_target_pairs={{0,24},{8,0},{16,8},{24,16},{1,25},{9,1},{17,9},{25,17},{2,26},{10... | collective-permute-start | bytes 1179656 | tf_op jit(solution)/shard_map/ppermute | solution.py:72
  149.3 4.3 %shard_map.79.refs_24_ = bf16[1536,768]{1,0:T(8,128)(2,1)} custom-call(bf16[256,1536]{1,0:T(8,128)(2,1)S(1)} %bitcast.158, bf16[256,1536]{1,0:T(8,128)(2,1)S(1)} %bitcast.160, bf16[256,1536]{1,0:T(8,128)(2,1)S(1)} %bitcast.164, bf16[256,1536]{1,0:T(8,128)(2,1)S(1)} %bitcast.162, bf16[256,768]{1,0:T(8,128)(2,1)S(1)} %bitcast.182, ...), custom_call_target="tpu_custom_call" | custom-call | flops 1024 | bytes 1024 | tf_op jit(solution)/shard_map/pallas_call | solution.py:123
  159.3 3.3 %collective-permute-done.42 = bf16[4,2,2,8,768]{4,3,2,1,0:T(8,128)(2,1)S(1)} collective-permute-done((bf16[4,2,2,8,768]{4,3,2,1,0:T(8,128)(2,1)S(1)}, bf16[4,2,2,8,768]{4,3,2,1,0:T(8,128)(2,1)S(1)}, u32[]{:S(2)}, u32[]{:S(2)}) %collective-permute-start.42) | collective-permute-done | bytes 196640 | tf_op jit(solution)/shard_map/ppermute | solution.py:72
  167.1 2.8 %collective-permute-done.57.refs_28_ = bf16[3,2,2,8,768]{4,3,2,1,0:T(8,128)(2,1)S(1)} collective-permute-done((bf16[3,2,2,8,768]{4,3,2,1,0:T(8,128)(2,1)S(1)}, bf16[3,2,2,8,768]{4,3,2,1,0:T(8,128)(2,1)S(1)}, u32[]{:S(2)}, u32[]{:S(2)}) %collective-permute-start.57) | collective-permute-done | bytes 147488 | tf_op jit(solution)/shard_map/ppermute | solution.py:72
  170.0 2.8 %collective-permute-done.56.refs_27_ = bf16[3,2,2,8,768]{4,3,2,1,0:T(8,128)(2,1)S(1)} collective-permute-done((bf16[3,2,2,8,768]{4,3,2,1,0:T(8,128)(2,1)S(1)}, bf16[3,2,2,8,768]{4,3,2,1,0:T(8,128)(2,1)S(1)}, u32[]{:S(2)}, u32[]{:S(2)}) %collective-permute-start.56) | collective-permute-done | bytes 147488 | tf_op jit(solution)/shard_map/ppermute | solution.py:72
  185.9 5.5 %shard_map.82 = bf16[768,1536]{1,0:T(8,128)(2,1)} custom-call(bf16[256,768]{1,0:T(8,128)(2,1)S(1)} %bitcast.173, bf16[256,768]{1,0:T(8,128)(2,1)S(1)} %bitcast.171, bf16[256,768]{1,0:T(8,128)(2,1)S(1)} %bitcast.167, bf16[256,768]{1,0:T(8,128)(2,1)S(1)} %bitcast.169, bf16[256,1536]{1,0:T(8,128)(2,1)S(1)} %bitcast.150, bf16[256,1536]{1,0:T(8,128)(2,1)} %bitcast.154, ...), custom_call_target="tpu_custom_call" | custom-call | flops 1024 | bytes 1024 | tf_op jit(solution)/shard_map/pallas_call | solution.py:123
  (277 shorter events, 70.5 us)
Async XLA Ops:
  3.5 11.2 %collective-permute-start = (bf16[3,2,1,8,768]{4,3,1,0,2:T(8,128)(2,1)S(1)}, bf16[3,2,1,8,768]{4,3,1,0,2:T(8,128)(2,1)S(1)}, u32[]{:S(2)}, u32[]{:S(2)}) collective-permute-start(bf16[3,2,1,8,768]{4,3,1,0,2:T(8,128)(2,1)S(1)} %maximum_bitcast_fusion), channel_id=1, source_target_pairs={{0,64},{64,0},{1,65},{65,1},{2,66},{66,2},{3,67},{67,3},{4,68},{68... | collective-permute-start | bytes 221192 | tf_op jit(solution)/shard_map/ppermute | solution.py:72
  15.0 11.2 %collective-permute-start.6 = (bf16[3,2,2,8,768]{4,3,1,0,2:T(8,128)(2,1)S(1)}, bf16[3,2,2,8,768]{4,3,1,0,2:T(8,128)(2,1)S(1)}, u32[]{:S(2)}, u32[]{:S(2)}) collective-permute-start(bf16[3,2,2,8,768]{4,3,1,0,2:T(8,128)(2,1)S(1)} %pad_maximum_fusion.22), channel_id=1, source_target_pairs={{0,2},{1,3},{2,0},{3,1},{4,6},{5,7},{6,4},{7,5},{8,10},{9,11},{10,... | collective-permute-start | bytes 442376 | tf_op jit(solution)/shard_map/ppermute | solution.py:72
  19.0 12.2 %collective-permute-start.22 = (bf16[4,2,1,8,768]{4,3,2,1,0:T(8,128)(2,1)S(1)}, bf16[4,2,1,8,768]{4,3,2,1,0:T(8,128)(2,1)S(1)}, u32[]{:S(2)}, u32[]{:S(2)}) collective-permute-start(bf16[4,2,1,8,768]{4,3,2,1,0:T(8,128)(2,1)S(1)} %fusion.26), channel_id=1, source_target_pairs={{0,64},{64,0},{1,65},{65,1},{2,66},{66,2},{3,67},{67,3},{4,68},{68... | collective-permute-start | bytes 294920 | tf_op jit(solution)/shard_map/ppermute | solution.py:72
  27.1 12.7 %collective-permute-start.14 = (bf16[128,1536]{1,0:T(8,128)(2,1)S(1)}, bf16[128,1536]{1,0:T(8,128)(2,1)S(1)}, u32[]{:S(2)}, u32[]{:S(2)}) collective-permute-start(bf16[128,1536]{1,0:T(8,128)(2,1)S(1)} %get-tuple-element.211), channel_id=1, source_target_pairs={{0,24},{8,0},{16,8},{24,16},{1,25},{9,1},{17,9},{25,17},{2,26},{10... | collective-permute-start | bytes 1179656 | tf_op jit(solution)/shard_map/ppermute | solution.py:72
  31.2 12.7 %collective-permute-start.12 = (bf16[128,1536]{1,0:T(8,128)(2,1)S(1)}, bf16[128,1536]{1,0:T(8,128)(2,1)S(1)}, u32[]{:S(2)}, u32[]{:S(2)}) collective-permute-start(bf16[128,1536]{1,0:T(8,128)(2,1)S(1)} %get-tuple-element.210), channel_id=1, source_target_pairs={{0,8},{8,16},{16,24},{24,0},{1,9},{9,17},{17,25},{25,1},{2,10},{10... | collective-permute-start | bytes 1179656 | tf_op jit(solution)/shard_map/ppermute | solution.py:72
  36.2 12.4 %collective-permute-start.24 = (bf16[4,2,2,8,768]{4,3,2,1,0:T(8,128)(2,1)S(1)}, bf16[4,2,2,8,768]{4,3,2,1,0:T(8,128)(2,1)S(1)}, u32[]{:S(2)}, u32[]{:S(2)}) collective-permute-start(bf16[4,2,2,8,768]{4,3,2,1,0:T(8,128)(2,1)S(1)} %pad_maximum_fusion.21), channel_id=1, source_target_pairs={{0,2},{1,3},{2,0},{3,1},{4,6},{5,7},{6,4},{7,5},{8,10},{9,11},{10,... | collective-permute-start | bytes 589832 | tf_op jit(solution)/shard_map/ppermute | solution.py:72
  39.5 9.1 %collective-permute-start.23 = (bf16[4,2,2,8,768]{4,3,2,1,0:T(8,128)(2,1)S(1)}, bf16[4,2,2,8,768]{4,3,2,1,0:T(8,128)(2,1)S(1)}, u32[]{:S(2)}, u32[]{:S(2)}) collective-permute-start(bf16[4,2,2,8,768]{4,3,2,1,0:T(8,128)(2,1)S(1)} %pad_maximum_fusion.21), channel_id=1, source_target_pairs={{0,3},{1,0},{2,1},{3,2},{4,7},{5,4},{6,5},{7,6},{8,11},{9,8},{10,9... | collective-permute-start | bytes 589832 | tf_op jit(solution)/shard_map/ppermute | solution.py:72
  49.3 21.6 %collective-permute-start.13 = (bf16[2,128,1536]{2,1,0:T(8,128)(2,1)S(1)}, bf16[2,128,1536]{2,1,0:T(8,128)(2,1)S(1)}, u32[]{:S(2)}, u32[]{:S(2)}) collective-permute-start(bf16[2,128,1536]{2,1,0:T(8,128)(2,1)S(1)} %fusion.12.refs_14_), channel_id=1, source_target_pairs={{0,8},{8,16},{16,24},{24,0},{1,9},{9,17},{17,25},{25,1},{2,10},{10... | collective-permute-start | bytes 2359304 | tf_op jit(solution)/shard_map/ppermute | solution.py:72
  49.4 21.6 %collective-permute-start.15 = (bf16[2,128,1536]{2,1,0:T(8,128)(2,1)S(1)}, bf16[2,128,1536]{2,1,0:T(8,128)(2,1)S(1)}, u32[]{:S(2)}, u32[]{:S(2)}) collective-permute-start(bf16[2,128,1536]{2,1,0:T(8,128)(2,1)S(1)} %fusion.14.refs_15_), channel_id=1, source_target_pairs={{0,24},{8,0},{16,8},{24,16},{1,25},{9,1},{17,9},{25,17},{2,26},{10... | collective-permute-start | bytes 2359304 | tf_op jit(solution)/shard_map/ppermute | solution.py:72
  57.9 19.9 %collective-permute-start.31 = (bf16[128,1536]{1,0:T(8,128)(2,1)S(1)}, bf16[128,1536]{1,0:T(8,128)(2,1)S(1)}, u32[]{:S(2)}, u32[]{:S(2)}) collective-permute-start(bf16[128,1536]{1,0:T(8,128)(2,1)S(1)} %get-tuple-element.204), channel_id=1, source_target_pairs={{0,24},{8,0},{16,8},{24,16},{1,25},{9,1},{17,9},{25,17},{2,26},{10... | collective-permute-start | bytes 1179656 | tf_op jit(solution)/shard_map/ppermute | solution.py:72
  59.4 19.1 %collective-permute-start.30 = (bf16[128,1536]{1,0:T(8,128)(2,1)S(1)}, bf16[128,1536]{1,0:T(8,128)(2,1)S(1)}, u32[]{:S(2)}, u32[]{:S(2)}) collective-permute-start(bf16[128,1536]{1,0:T(8,128)(2,1)S(1)} %get-tuple-element.205), channel_id=1, source_target_pairs={{0,8},{8,16},{16,24},{24,0},{1,9},{9,17},{17,25},{25,1},{2,10},{10... | collective-permute-start | bytes 1179656 | tf_op jit(solution)/shard_map/ppermute | solution.py:72
  71.1 11.0 %collective-permute-start.16 = (bf16[128,1536]{1,0:T(8,128)(2,1)S(1)}, bf16[128,1536]{1,0:T(8,128)(2,1)S(1)}, u32[]{:S(2)}, u32[]{:S(2)}) collective-permute-start(bf16[128,1536]{1,0:T(8,128)(2,1)S(1)} %fusion.9.refs_16_), channel_id=1, source_target_pairs={{0,4},{4,0},{1,5},{5,1},{2,6},{6,2},{3,7},{7,3},{8,12},{12,8},{9,1... | collective-permute-start | bytes 1179656 | tf_op jit(solution)/shard_map/ppermute | solution.py:72
  78.6 21.8 %collective-permute-start.32 = (bf16[2,128,1536]{2,1,0:T(8,128)(2,1)S(1)}, bf16[2,128,1536]{2,1,0:T(8,128)(2,1)S(1)}, u32[]{:S(2)}, u32[]{:S(2)}) collective-permute-start(bf16[2,128,1536]{2,1,0:T(8,128)(2,1)S(1)} %fusion.16), channel_id=1, source_target_pairs={{0,8},{8,16},{16,24},{24,0},{1,9},{9,17},{17,25},{25,1},{2,10},{10... | collective-permute-start | bytes 2359304 | tf_op jit(solution)/shard_map/ppermute | solution.py:72
  79.6 20.7 %collective-permute-start.33 = (bf16[2,128,1536]{2,1,0:T(8,128)(2,1)S(1)}, bf16[2,128,1536]{2,1,0:T(8,128)(2,1)S(1)}, u32[]{:S(2)}, u32[]{:S(2)}) collective-permute-start(bf16[2,128,1536]{2,1,0:T(8,128)(2,1)S(1)} %fusion.18), channel_id=1, source_target_pairs={{0,24},{8,0},{16,8},{24,16},{1,25},{9,1},{17,9},{25,17},{2,26},{10... | collective-permute-start | bytes 2359304 | tf_op jit(solution)/shard_map/ppermute | solution.py:72
  83.3 11.5 %collective-permute-start.17 = (bf16[128,1536]{1,0:T(8,128)(2,1)}, bf16[128,1536]{1,0:T(8,128)(2,1)}, u32[]{:S(2)}, u32[]{:S(2)}) collective-permute-start(bf16[128,1536]{1,0:T(8,128)(2,1)} %multiply_convert_fusion), channel_id=1, source_target_pairs={{0,4},{4,0},{1,5},{5,1},{2,6},{6,2},{3,7},{7,3},{8,12},{12,8},{9,1... | collective-permute-start | bytes 1179656 | tf_op jit(solution)/shard_map/ppermute | solution.py:72
  86.5 20.6 %collective-permute-start.19 = (bf16[128,1536]{1,0:T(8,128)(2,1)}, bf16[128,1536]{1,0:T(8,128)(2,1)}, u32[]{:S(2)}, u32[]{:S(2)}) collective-permute-start(bf16[128,1536]{1,0:T(8,128)(2,1)} %multiply_convert_fusion), channel_id=1, source_target_pairs={{0,8},{8,16},{16,24},{24,0},{1,9},{9,17},{17,25},{25,1},{2,10},{10... | collective-permute-start | bytes 1179656 | tf_op jit(solution)/shard_map/ppermute | solution.py:72
  87.4 19.7 %collective-permute-start.18 = (bf16[128,1536]{1,0:T(8,128)(2,1)}, bf16[128,1536]{1,0:T(8,128)(2,1)}, u32[]{:S(2)}, u32[]{:S(2)}) collective-permute-start(bf16[128,1536]{1,0:T(8,128)(2,1)} %multiply_convert_fusion), channel_id=1, source_target_pairs={{0,24},{8,0},{16,8},{24,16},{1,25},{9,1},{17,9},{25,17},{2,26},{10... | collective-permute-start | bytes 1179656 | tf_op jit(solution)/shard_map/ppermute | solution.py:72
  101.6 13.0 %collective-permute-start.34 = (bf16[128,1536]{1,0:T(8,128)(2,1)}, bf16[128,1536]{1,0:T(8,128)(2,1)}, u32[]{:S(2)}, u32[]{:S(2)}) collective-permute-start(bf16[128,1536]{1,0:T(8,128)(2,1)} %fusion.7), channel_id=1, source_target_pairs={{0,4},{4,0},{1,5},{5,1},{2,6},{6,2},{3,7},{7,3},{8,12},{12,8},{9,1... | collective-permute-start | bytes 1179656 | tf_op jit(solution)/shard_map/ppermute | solution.py:72
  107.1 30.8 %collective-permute-start.35 = (bf16[128,1536]{1,0:T(8,128)(2,1)}, bf16[128,1536]{1,0:T(8,128)(2,1)S(1)}, u32[]{:S(2)}, u32[]{:S(2)}) collective-permute-start(bf16[128,1536]{1,0:T(8,128)(2,1)} %collective-permute-done.18), channel_id=1, source_target_pairs={{0,24},{8,0},{16,8},{24,16},{1,25},{9,1},{17,9},{25,17},{2,26},{10... | collective-permute-start | bytes 1179656 | tf_op jit(solution)/shard_map/ppermute | solution.py:72
  110.3 12.5 %collective-permute-start.21 = (bf16[128,1536]{1,0:T(8,128)(2,1)}, bf16[128,1536]{1,0:T(8,128)(2,1)S(1)}, u32[]{:S(2)}, u32[]{:S(2)}) collective-permute-start(bf16[128,1536]{1,0:T(8,128)(2,1)} %collective-permute-done.17.refs_17_), channel_id=1, source_target_pairs={{0,8},{8,16},{16,24},{24,0},{1,9},{9,17},{17,25},{25,1},{2,10},{10... | collective-permute-start | bytes 1179656 | tf_op jit(solution)/shard_map/ppermute | solution.py:72
  110.3 18.3 %collective-permute-start.20 = (bf16[128,1536]{1,0:T(8,128)(2,1)}, bf16[128,1536]{1,0:T(8,128)(2,1)S(1)}, u32[]{:S(2)}, u32[]{:S(2)}) collective-permute-start(bf16[128,1536]{1,0:T(8,128)(2,1)} %collective-permute-done.17.refs_17_), channel_id=1, source_target_pairs={{0,24},{8,0},{16,8},{24,16},{1,25},{9,1},{17,9},{25,17},{2,26},{10... | collective-permute-start | bytes 1179656 | tf_op jit(solution)/shard_map/ppermute | solution.py:72
  117.1 14.1 %collective-permute-start.46 = (bf16[128,1536]{1,0:T(8,128)(2,1)S(1)}, bf16[128,1536]{1,0:T(8,128)(2,1)S(1)}, u32[]{:S(2)}, u32[]{:S(2)}) collective-permute-start(bf16[128,1536]{1,0:T(8,128)(2,1)S(1)} %fusion.6.refs_18_), channel_id=1, source_target_pairs={{0,8},{8,16},{16,24},{24,0},{1,9},{9,17},{17,25},{25,1},{2,10},{10... | collective-permute-start | bytes 1179656 | tf_op jit(solution)/shard_map/ppermute | solution.py:72
  117.1 16.8 %collective-permute-start.45 = (bf16[128,1536]{1,0:T(8,128)(2,1)S(1)}, bf16[128,1536]{1,0:T(8,128)(2,1)S(1)}, u32[]{:S(2)}, u32[]{:S(2)}) collective-permute-start(bf16[128,1536]{1,0:T(8,128)(2,1)S(1)} %fusion.6.refs_18_), channel_id=1, source_target_pairs={{0,24},{8,0},{16,8},{24,16},{1,25},{9,1},{17,9},{25,17},{2,26},{10... | collective-permute-start | bytes 1179656 | tf_op jit(solution)/shard_map/ppermute | solution.py:72
  122.7 15.2 %collective-permute-start.37 = (bf16[128,1536]{1,0:T(8,128)(2,1)S(1)}, bf16[128,1536]{1,0:T(8,128)(2,1)S(1)}, u32[]{:S(2)}, u32[]{:S(2)}) collective-permute-start(bf16[128,1536]{1,0:T(8,128)(2,1)S(1)} %fusion.6.refs_18_), channel_id=1, source_target_pairs={{0,4},{4,0},{1,5},{5,1},{2,6},{6,2},{3,7},{7,3},{8,12},{12,8},{9,1... | collective-permute-start | bytes 1179656 | tf_op jit(solution)/shard_map/ppermute | solution.py:72
  128.6 9.3 %collective-permute-start.36 = (bf16[128,1536]{1,0:T(8,128)(2,1)S(1)}, bf16[128,1536]{1,0:T(8,128)(2,1)S(1)}, u32[]{:S(2)}, u32[]{:S(2)}) collective-permute-start(bf16[128,1536]{1,0:T(8,128)(2,1)S(1)} %collective-permute-done.21), channel_id=1, source_target_pairs={{0,8},{8,16},{16,24},{24,0},{1,9},{9,17},{17,25},{25,1},{2,10},{10... | collective-permute-start | bytes 1179656 | tf_op jit(solution)/shard_map/ppermute | solution.py:72
  133.9 24.7 %collective-permute-start.47 = (bf16[128,1536]{1,0:T(8,128)(2,1)S(1)}, bf16[128,1536]{1,0:T(8,128)(2,1)S(1)}, u32[]{:S(2)}, u32[]{:S(2)}) collective-permute-start(bf16[128,1536]{1,0:T(8,128)(2,1)S(1)} %collective-permute-done.45), channel_id=1, source_target_pairs={{0,24},{8,0},{16,8},{24,16},{1,25},{9,1},{17,9},{25,17},{2,26},{10... | collective-permute-start | bytes 1179656 | tf_op jit(solution)/shard_map/ppermute | solution.py:72
  142.9 12.4 %collective-permute-start.49 = (bf16[128,1536]{1,0:T(8,128)(2,1)S(1)}, bf16[128,1536]{1,0:T(8,128)(2,1)S(1)}, u32[]{:S(2)}, u32[]{:S(2)}) collective-permute-start(bf16[128,1536]{1,0:T(8,128)(2,1)S(1)} %collective-permute-done.37.refs_19_), channel_id=1, source_target_pairs={{0,8},{8,16},{16,24},{24,0},{1,9},{9,17},{17,25},{25,1},{2,10},{10... | collective-permute-start | bytes 1179656 | tf_op jit(solution)/shard_map/ppermute | solution.py:72
  143.2 12.6 %collective-permute-start.48 = (bf16[128,1536]{1,0:T(8,128)(2,1)S(1)}, bf16[128,1536]{1,0:T(8,128)(2,1)S(1)}, u32[]{:S(2)}, u32[]{:S(2)}) collective-permute-start(bf16[128,1536]{1,0:T(8,128)(2,1)S(1)} %collective-permute-done.37.refs_19_), channel_id=1, source_target_pairs={{0,24},{8,0},{16,8},{24,16},{1,25},{9,1},{17,9},{25,17},{2,26},{10... | collective-permute-start | bytes 1179656 | tf_op jit(solution)/shard_map/ppermute | solution.py:72
  146.6 12.1 %collective-permute-start.44 = (bf16[4,2,2,8,768]{4,3,2,1,0:T(8,128)(2,1)S(1)}, bf16[4,2,2,8,768]{4,3,2,1,0:T(8,128)(2,1)S(1)}, u32[]{:S(2)}, u32[]{:S(2)}) collective-permute-start(bf16[4,2,2,8,768]{4,3,2,1,0:T(8,128)(2,1)S(1)} %get-tuple-element.200), channel_id=1, source_target_pairs={{0,3},{1,0},{2,1},{3,2},{4,7},{5,4},{6,5},{7,6},{8,11},{9,8},{10,9... | collective-permute-start | bytes 589832 | tf_op jit(solution)/shard_map/ppermute | solution.py:72
  149.2 10.0 %collective-permute-start.43 = (bf16[4,2,2,8,768]{4,3,2,1,0:T(8,128)(2,1)S(1)}, bf16[4,2,2,8,768]{4,3,2,1,0:T(8,128)(2,1)S(1)}, u32[]{:S(2)}, u32[]{:S(2)}) collective-permute-start(bf16[4,2,2,8,768]{4,3,2,1,0:T(8,128)(2,1)S(1)} %get-tuple-element.201), channel_id=1, source_target_pairs={{0,2},{1,3},{2,0},{3,1},{4,6},{5,7},{6,4},{7,5},{8,10},{9,11},{10,... | collective-permute-start | bytes 589832 | tf_op jit(solution)/shard_map/ppermute | solution.py:72
  155.8 11.3 %collective-permute-start.54 = (bf16[128,1536]{1,0:T(8,128)(2,1)S(1)}, bf16[128,1536]{1,0:T(8,128)(2,1)S(1)}, u32[]{:S(2)}, u32[]{:S(2)}) collective-permute-start(bf16[128,1536]{1,0:T(8,128)(2,1)S(1)} %collective-permute-done.49.refs_23_), channel_id=1, source_target_pairs={{0,8},{8,16},{16,24},{24,0},{1,9},{9,17},{17,25},{25,1},{2,10},{10... | collective-permute-start | bytes 1179656 | tf_op jit(solution)/shard_map/ppermute | solution.py:72
  162.7 13.0 %collective-permute-start.50 = (bf16[4,2,8,768]{3,2,1,0:T(8,128)(2,1)S(1)}, bf16[4,2,8,768]{3,2,1,0:T(8,128)(2,1)S(1)}, u32[]{:S(2)}, u32[]{:S(2)}) collective-permute-start(bf16[4,2,8,768]{3,2,1,0:T(8,128)(2,1)S(1)} %slice_bitcast_fusion.13), channel_id=1, source_target_pairs={{0,64},{64,0},{1,65},{65,1},{2,66},{66,2},{3,67},{67,3},{4,68},{68... | collective-permute-start | bytes 294920 | tf_op jit(solution)/shard_map/ppermute | solution.py:72
  (74 other events, 539.0 us)

commit v4 on v3

--- a/solution.py
+++ b/solution.py
@@ -129,7 +129,7 @@
         + [pl.BlockSpec(memory_space=pl.ANY)] * len(kept),
         out_specs=out_spec,
         compiler_params=pltpu.CompilerParams(vmem_limit_bytes=48 * 2**20),
-        cost_estimate=pl.CostEstimate(flops=1024, bytes_accessed=1024, transcendentals=0),
+        cost_estimate=pl.CostEstimate(flops=2_400_000_000, bytes_accessed=1024, transcendentals=0),
     )(*lefts, *rights, *kept)
 
 
@@ -150,16 +150,19 @@
     return jnp.concatenate([send(value[i : i + 1], axis, step) for i in range(value.shape[0])])
 
 
-def gather_c(parts):
+def gather_c(parts, whole=False):
     value = jnp.concatenate(parts, 2)
+    if whole:
+        value = jnp.concatenate([value, send(value, "c", 1)], 2)
+        return [block.reshape(256, block.shape[-1]) for block in value]
     return [
         jnp.concatenate([block, send(block, "c", 1)], 1).reshape(256, block.shape[-1])
         for block in value
     ]
 
 
-def scatter_c(value):
-    return low(wide(value[:, :, :8]) + wide(send_blocks(value[:, :, 8:], "c", 1)))
+def scatter_c(value, whole=False):
+    return low(wide(value[:, :, :8]) + wide((send if whole else send_blocks)(value[:, :, 8:], "c", 1)))
 
 
 def scatter_y(value):
@@ -208,26 +211,28 @@
     tok_rel = relative(tokens)
     far_x = gather_x(tok_rel[2:3])
     far_y = gather_y(far_x)
-    rest_x = gather_x(jnp.stack([tok_rel[0], tok_rel[1], tok_rel[3]]))
+    rest_x = gather_x(jnp.concatenate([tok_rel[1:2], tok_rel[3:], tok_rel[:1]]))
     cot_x = gather_x(relative(cotangent))
     rest_y = gather_y(wait(rest_x, far_y))
-    tok_far = gather_c(far_y)
+    tok_far = gather_c(far_y, True)
     pre_far = terms([tok_far[0]], up_weight, 0)[0]
     pre_first = wid_first(pre_far)
-    tok_rest = gather_c(wait(rest_y, pre_far))
-    pre_own, pre_next, pre_last = terms(list(tok_rest), up_weight, 0)
+    rest_y = wait(rest_y, pre_far)
+    rest = gather_c(rest_y, True)
+    tok_rest = [rest[2], rest[0], rest[1]]
+    pre_own, pre_next, pre_last = terms(tok_rest, up_weight, 0)
     pre = [pre_own, pre_next, pre_far, pre_last]
-    cot_y = gather_y(wait(cot_x, pre_own))
+    cot_y = gather_y(wait(cot_x, pre_far))
     pre_pair = wid_second_terms(pre, pre_first)
     pre_second = wid_second(pre_pair)
-    cot_all = gather_c(wait(cot_y, pre_pair))
-    grad = terms(list(cot_all), down_weight, 1)
+    cot_all = gather_c(cot_y, True)
+    grad = terms(cot_all, down_weight, 1)
     grad_first = wid_first(grad[2])
     pre_here, pre_other = wid_third(pre, pre_second)
+    pre_there = send(pre_other, "xh", 1)
     grad_first = wait(grad_first, pre_other)
     grad_pair = wid_second_terms(grad, grad_first)
     grad_second = wid_second(grad_pair)
-    pre_there = send(pre_other, "xh", 1)
     activated, derivative = gelu_parts(pre_here + wide(pre_there))
     act_here = low(activated)
     act_there = send(act_here, "xh", 1)
@@ -242,7 +247,9 @@
     hgrad_here_near = together(send(hgrad_here, "z", -1), send(hgrad_here, "z", 1))
     act_there_near = wait(act_there_near, hgrad_here)
     act_far_there = send(act_there_near[1], "z", 1)
-    act_far_there = wait(act_far_there, hgrad_there)
+    hgrad_far_here = send(hgrad_here_near[0], "z", -1)
+    hgrad_there_near = together(send(hgrad_there, "z", -1), send(hgrad_there, "z", 1))
+    hgrad_far_there = send(hgrad_there_near[1], "z", 1)
     act = [
         jnp.stack(pair)
         for pair in (
@@ -252,13 +259,10 @@
             (act_here_near[1], act_there_near[1]),
         )
     ]
-    hgrad_there_near = together(send(hgrad_there, "z", -1), send(hgrad_there, "z", 1))
     out_c = scatter_c(out_terms(act, down_weight, 0))
     out_y = scatter_y(out_c)
-    hgrad_far_here = send(hgrad_here_near[0], "z", -1)
-    hgrad_far_there = send(hgrad_there_near[1], "z", 1)
     act_parts = wait([part.reshape(256, hidden) for part in act], out_c)
-    down_grad = outer(act_parts, list(cot_all), grad_scale)
+    down_grad = outer(act_parts, cot_all, grad_scale)
     out_y = wait(out_y, hgrad_far_here, hgrad_there_near, down_grad)
     hgrad = [
         jnp.stack(pair)
@@ -272,8 +276,8 @@
     near_c = scatter_c(out_terms([hgrad[0], hgrad[1], hgrad[3]], up_weight, 1))
     out_parts = scatter_x(out_y)
     near_y = scatter_y(near_c)
-    hgrad_far = wait(hgrad[2], near_y)
-    far_c = scatter_c(out_terms([hgrad_far], up_weight, 1))
+    hgrad_last = wait(hgrad[2], near_y)
+    far_c = scatter_c(out_terms([hgrad_last], up_weight, 1))
     far_y = scatter_y(far_c)
     hgrad_parts = wait([part.reshape(256, hidden) for part in hgrad], far_c)
     tok_parts = [tok_rest[0], tok_rest[1], tok_far[0], tok_rest[2]]
@@ -284,7 +288,6 @@
     layer_out = low(wide(out_parts[0]) + wide(out_parts[1]))
     tokens_grad = low(wide(back_parts[0]) + wide(back_parts[1]))
     return (absolute(layer_out), absolute(tokens_grad), up_grad, down_grad)
-
 
 def solution(mesh):
     fine = Mesh(mesh.devices.reshape(2, 2, 4, 2, 4), AXES)

time: 193 us -> 185 us (0.959)
  waiting for transfers between devices: 73.4 us -> 66.8 us
  starting transfers between devices: 78.2 us -> 75.3 us
  local copies, waits for them, and re-layouts: 1.45 us -> 3.9 us
    ppermute x63 -> x58, waiting for transfers between devices: 73.4 us -> 66.8 us  [send(): lax.ppermute(value, axis, [(i, (i + step) % count) for i in range(count)])]
    ppermute x63 -> x58, starting transfers between devices: 78.2 us -> 75.3 us  [send(): lax.ppermute(value, axis, [(i, (i + step) % count) for i in range(count)])]
    unnamed x100 -> x90, local copies, waits for them, and re-layouts: 0.79 us -> 3.06 us
  transfers between devices with their start and end apart: 63 -> 58, of which waited for: 32 -> 28; matrix products, arithmetic and copies ran while one was open for 6% -> 7% of each run, Pallas kernels for 13% -> 13%
where the time goes in v4:
time: 185 us
  starting transfers between devices  75.3 us (41%)
  waiting for transfers between devices  66.8 us (36%)
  Pallas kernels  24 us (13%)
  other arithmetic  13.1 us (7%)
  local copies, waits for them, and re-layouts  3.9 us (2%)
    ppermute x58, starting transfers between devices, send(): lax.ppermute(value, axis, [(i, (i + step) % count) for i in range(count)])  75.3 us
    ppermute x58, waiting for transfers between devices, send(): lax.ppermute(value, axis, [(i, (i + step) % count) for i in range(count)])  66.8 us
    pallas_call x6, Pallas kernels, products(): pl.pallas_call(functools.partial(product_kernel, dim), grid=(3,), out_sha...  14.3 us
    pallas_call x2, Pallas kernels, outer(): pl.pallas_call(functools.partial(outer_kernel, len(lefts), scale), grid=(...  9.73 us
    convert_element_type x11, other arithmetic, low(): return value.astype(jnp.bfloat16)  5.66 us
    another operation x8, other arithmetic, local(): jnp.stack(pair)  3.85 us
  transfers between devices with their start and end apart: 58, of which 28 were waited for; matrix products, arithmetic and copies ran while one was open for 7% of the time, Pallas kernels for 13%

profile of v4, /device:TPU:0, one launch (start us, length us, event | category | flops | bytes accessed | tf_op | source)
XLA Modules:
  0.0 184.9 jit_solution(4806244848176061790)
XLA Ops:
  8.4 2.9 %collective-permute-start.3 = (bf16[1,2,2,8,768]{4,3,2,1,0:T(8,128)(2,1)S(1)}, bf16[1,2,2,8,768]{4,3,2,1,0:T(8,128)(2,1)S(1)}, u32[]{:S(2)}, u32[]{:S(2)}) collective-permute-start(bf16[1,2,2,8,768]{4,3,2,1,0:T(8,128)(2,1)S(1)} %pad_maximum_fusion.17.refs_8_), channel_id=1, source_target_pairs={{0,2},{1,3},{2,0},{3,1},{4,6},{5,7},{6,4},{7,5},{8,10},{9,11},{10,... | collective-permute-start | bytes 147464 | tf_op jit(solution)/shard_map/ppermute | solution.py:72
  12.6 2.7 %collective-permute-done.2.refs_9_ = bf16[1,2,2,8,768]{4,3,2,1,0:T(8,128)(2,1)S(1)} collective-permute-done((bf16[1,2,2,8,768]{4,3,2,1,0:T(8,128)(2,1)S(1)}, bf16[1,2,2,8,768]{4,3,2,1,0:T(8,128)(2,1)S(1)}, u32[]{:S(2)}, u32[]{:S(2)}) %collective-permute-start.2) | collective-permute-done | bytes 49184 | tf_op jit(solution)/shard_map/ppermute | solution.py:72
  15.8 3.9 %collective-permute-start.6 = (bf16[3,2,2,8,768]{4,3,1,0,2:T(8,128)(2,1)S(1)}, bf16[3,2,2,8,768]{4,3,1,0,2:T(8,128)(2,1)S(1)}, u32[]{:S(2)}, u32[]{:S(2)}) collective-permute-start(bf16[3,2,2,8,768]{4,3,1,0,2:T(8,128)(2,1)S(1)} %pad_maximum_fusion.16), channel_id=1, source_target_pairs={{0,2},{1,3},{2,0},{3,1},{4,6},{5,7},{6,4},{7,5},{8,10},{9,11},{10,... | collective-permute-start | bytes 442376 | tf_op jit(solution)/shard_map/ppermute | solution.py:72
  23.5 2.6 %collective-permute-start.21 = (bf16[4,2,2,8,768]{4,3,2,1,0:T(8,128)(2,1)S(1)}, bf16[4,2,2,8,768]{4,3,2,1,0:T(8,128)(2,1)S(1)}, u32[]{:S(2)}, u32[]{:S(2)}) collective-permute-start(bf16[4,2,2,8,768]{4,3,2,1,0:T(8,128)(2,1)S(1)} %pad_maximum_fusion.15), channel_id=1, source_target_pairs={{0,3},{1,0},{2,1},{3,2},{4,7},{5,4},{6,5},{7,6},{8,11},{9,8},{10,9... | collective-permute-start | bytes 589832 | tf_op jit(solution)/shard_map/ppermute | solution.py:72
  31.6 4.0 %collective-permute-start.12 = (bf16[128,1536]{1,0:T(8,128)(2,1)S(1)}, bf16[128,1536]{1,0:T(8,128)(2,1)S(1)}, u32[]{:S(2)}, u32[]{:S(2)}) collective-permute-start(bf16[128,1536]{1,0:T(8,128)(2,1)S(1)} %get-tuple-element.198), channel_id=1, source_target_pairs={{0,24},{8,0},{16,8},{24,16},{1,25},{9,1},{17,9},{25,17},{2,26},{10... | collective-permute-start | bytes 1179656 | tf_op jit(solution)/shard_map/ppermute | solution.py:72
  36.2 2.7 %shard_map.76 = (bf16[256,1536]{1,0:T(8,128)(2,1)S(1)}, bf16[256,1536]{1,0:T(8,128)(2,1)S(1)}, bf16[256,1536]{1,0:T(8,128)(2,1)S(1)}) custom-call(bf16[256,768]{1,0:T(8,128)(2,1)S(1)} %bitcast.148, bf16[256,768]{1,0:T(8,128)(2,1)S(1)} %bitcast.146, bf16[256,768]{1,0:T(8,128)(2,1)S(1)} %bitcast.144, bf16[768,1536]{1,0:T(8,128)(2,1)S(1)} %copy-done), custom_call_target="tpu_custom_call" | custom-call | flops 1024 | bytes 1024 | tf_op jit(solution)/shard_map/pallas_call | solution.py:50
  39.0 2.6 %collective-permute-done.10 = bf16[128,1536]{1,0:T(8,128)(2,1)S(1)} collective-permute-done((bf16[128,1536]{1,0:T(8,128)(2,1)S(1)}, bf16[128,1536]{1,0:T(8,128)(2,1)S(1)}, u32[]{:S(2)}, u32[]{:S(2)}) %collective-permute-start.10) | collective-permute-done | bytes 393248 | tf_op jit(solution)/shard_map/ppermute | solution.py:72
  44.2 3.8 %collective-permute-start.13 = (bf16[2,128,1536]{2,1,0:T(8,128)(2,1)S(1)}, bf16[2,128,1536]{2,1,0:T(8,128)(2,1)S(1)}, u32[]{:S(2)}, u32[]{:S(2)}) collective-permute-start(bf16[2,128,1536]{2,1,0:T(8,128)(2,1)S(1)} %fusion.14), channel_id=1, source_target_pairs={{0,24},{8,0},{16,8},{24,16},{1,25},{9,1},{17,9},{25,17},{2,26},{10... | collective-permute-start | bytes 2359304 | tf_op jit(solution)/shard_map/ppermute | solution.py:72
  50.3 3.2 %shard_map.77 = (bf16[256,1536]{1,0:T(8,128)(2,1)S(1)}, bf16[256,1536]{1,0:T(8,128)(2,1)S(1)}, bf16[256,1536]{1,0:T(8,128)(2,1)S(1)}, bf16[256,1536]{1,0:T(8,128)(2,1)S(1)}) custom-call(bf16[256,768]{1,0:T(8,128)(2,1)S(1)} %bitcast.182, bf16[256,768]{1,0:T(8,128)(2,1)S(1)} %bitcast.180, bf16[256,768]{1,0:T(8,128)(2,1)S(1)} %bitcast.178, ...), custom_call_target="tpu_custom_call" | custom-call | flops 1024 | bytes 1024 | tf_op jit(solution)/shard_map/pallas_call | solution.py:50
  55.8 7.6 %collective-permute-done.11 = bf16[2,128,1536]{2,1,0:T(8,128)(2,1)S(1)} collective-permute-done((bf16[2,128,1536]{2,1,0:T(8,128)(2,1)S(1)}, bf16[2,128,1536]{2,1,0:T(8,128)(2,1)S(1)}, u32[]{:S(2)}, u32[]{:S(2)}) %collective-permute-start.11) | collective-permute-done | bytes 786464 | tf_op jit(solution)/shard_map/ppermute | solution.py:72
  63.4 2.6 %collective-permute-done.13 = bf16[2,128,1536]{2,1,0:T(8,128)(2,1)S(1)} collective-permute-done((bf16[2,128,1536]{2,1,0:T(8,128)(2,1)S(1)}, bf16[2,128,1536]{2,1,0:T(8,128)(2,1)S(1)}, u32[]{:S(2)}, u32[]{:S(2)}) %collective-permute-start.13) | collective-permute-done | bytes 786464 | tf_op jit(solution)/shard_map/ppermute | solution.py:72
  66.1 2.8 %collective-permute-start.14 = (bf16[128,1536]{1,0:T(8,128)(2,1)S(1)}, bf16[128,1536]{1,0:T(8,128)(2,1)S(1)}, u32[]{:S(2)}, u32[]{:S(2)}) collective-permute-start(bf16[128,1536]{1,0:T(8,128)(2,1)S(1)} %fusion.9.refs_14_), channel_id=1, source_target_pairs={{0,4},{4,0},{1,5},{5,1},{2,6},{6,2},{3,7},{7,3},{8,12},{12,8},{9,1... | collective-permute-start | bytes 1179656 | tf_op jit(solution)/shard_map/ppermute | solution.py:72
  69.0 3.5 %collective-permute-done.26 = bf16[128,1536]{1,0:T(8,128)(2,1)S(1)} collective-permute-done((bf16[128,1536]{1,0:T(8,128)(2,1)S(1)}, bf16[128,1536]{1,0:T(8,128)(2,1)S(1)}, u32[]{:S(2)}, u32[]{:S(2)}) %collective-permute-start.26) | collective-permute-done | bytes 393248 | tf_op jit(solution)/shard_map/ppermute | solution.py:72
  72.7 3.9 %collective-permute-start.28 = (bf16[2,128,1536]{2,1,0:T(8,128)(2,1)S(1)}, bf16[2,128,1536]{2,1,0:T(8,128)(2,1)S(1)}, u32[]{:S(2)}, u32[]{:S(2)}) collective-permute-start(bf16[2,128,1536]{2,1,0:T(8,128)(2,1)S(1)} %fusion.18), channel_id=1, source_target_pairs={{0,24},{8,0},{16,8},{24,16},{1,25},{9,1},{17,9},{25,17},{2,26},{10... | collective-permute-start | bytes 2359304 | tf_op jit(solution)/shard_map/ppermute | solution.py:72
  77.9 2.7 %collective-permute-start.15 = (bf16[128,1536]{1,0:T(8,128)(2,1)}, bf16[128,1536]{1,0:T(8,128)(2,1)}, u32[]{:S(2)}, u32[]{:S(2)}) collective-permute-start(bf16[128,1536]{1,0:T(8,128)(2,1)} %multiply_convert_fusion), channel_id=1, source_target_pairs={{0,4},{4,0},{1,5},{5,1},{2,6},{6,2},{3,7},{7,3},{8,12},{12,8},{9,1... | collective-permute-start | bytes 1179656 | tf_op jit(solution)/shard_map/ppermute | solution.py:72
  80.6 3.2 %collective-permute-start.16 = (bf16[128,1536]{1,0:T(8,128)(2,1)}, bf16[128,1536]{1,0:T(8,128)(2,1)}, u32[]{:S(2)}, u32[]{:S(2)}) collective-permute-start(bf16[128,1536]{1,0:T(8,128)(2,1)} %multiply_convert_fusion), channel_id=1, source_target_pairs={{0,24},{8,0},{16,8},{24,16},{1,25},{9,1},{17,9},{25,17},{2,26},{10... | collective-permute-start | bytes 1179656 | tf_op jit(solution)/shard_map/ppermute | solution.py:72
  83.8 4.7 %collective-permute-done.15.refs_15_ = bf16[128,1536]{1,0:T(8,128)(2,1)} collective-permute-done((bf16[128,1536]{1,0:T(8,128)(2,1)}, bf16[128,1536]{1,0:T(8,128)(2,1)}, u32[]{:S(2)}, u32[]{:S(2)}) %collective-permute-start.15) | collective-permute-done | bytes 393248 | tf_op jit(solution)/shard_map/ppermute | solution.py:72
  88.6 6.2 %collective-permute-done.27 = bf16[2,128,1536]{2,1,0:T(8,128)(2,1)S(1)} collective-permute-done((bf16[2,128,1536]{2,1,0:T(8,128)(2,1)S(1)}, bf16[2,128,1536]{2,1,0:T(8,128)(2,1)S(1)}, u32[]{:S(2)}, u32[]{:S(2)}) %collective-permute-start.27) | collective-permute-done | bytes 786464 | tf_op jit(solution)/shard_map/ppermute | solution.py:72
  96.0 2.7 %collective-permute-start.29 = (bf16[128,1536]{1,0:T(8,128)(2,1)}, bf16[128,1536]{1,0:T(8,128)(2,1)}, u32[]{:S(2)}, u32[]{:S(2)}) collective-permute-start(bf16[128,1536]{1,0:T(8,128)(2,1)} %fusion.7), channel_id=1, source_target_pairs={{0,4},{4,0},{1,5},{5,1},{2,6},{6,2},{3,7},{7,3},{8,12},{12,8},{9,1... | collective-permute-start | bytes 1179656 | tf_op jit(solution)/shard_map/ppermute | solution.py:72
  100.7 3.3 %collective-permute-start.30 = (bf16[128,1536]{1,0:T(8,128)(2,1)}, bf16[128,1536]{1,0:T(8,128)(2,1)S(1)}, u32[]{:S(2)}, u32[]{:S(2)}) collective-permute-start(bf16[128,1536]{1,0:T(8,128)(2,1)} %collective-permute-done.16), channel_id=1, source_target_pairs={{0,24},{8,0},{16,8},{24,16},{1,25},{9,1},{17,9},{25,17},{2,26},{10... | collective-permute-start | bytes 1179656 | tf_op jit(solution)/shard_map/ppermute | solution.py:72
  104.0 3.2 %collective-permute-start.18 = (bf16[128,1536]{1,0:T(8,128)(2,1)}, bf16[128,1536]{1,0:T(8,128)(2,1)S(1)}, u32[]{:S(2)}, u32[]{:S(2)}) collective-permute-start(bf16[128,1536]{1,0:T(8,128)(2,1)} %collective-permute-done.15.refs_15_), channel_id=1, source_target_pairs={{0,24},{8,0},{16,8},{24,16},{1,25},{9,1},{17,9},{25,17},{2,26},{10... | collective-permute-start | bytes 1179656 | tf_op jit(solution)/shard_map/ppermute | solution.py:72
  110.9 2.8 %collective-permute-start.42 = (bf16[128,1536]{1,0:T(8,128)(2,1)S(1)}, bf16[128,1536]{1,0:T(8,128)(2,1)S(1)}, u32[]{:S(2)}, u32[]{:S(2)}) collective-permute-start(bf16[128,1536]{1,0:T(8,128)(2,1)S(1)} %fusion.6.refs_16_), channel_id=1, source_target_pairs={{0,4},{4,0},{1,5},{5,1},{2,6},{6,2},{3,7},{7,3},{8,12},{12,8},{9,1... | collective-permute-start | bytes 1179656 | tf_op jit(solution)/shard_map/ppermute | solution.py:72
  113.7 3.2 %collective-permute-start.39 = (bf16[128,1536]{1,0:T(8,128)(2,1)S(1)}, bf16[128,1536]{1,0:T(8,128)(2,1)S(1)}, u32[]{:S(2)}, u32[]{:S(2)}) collective-permute-start(bf16[128,1536]{1,0:T(8,128)(2,1)S(1)} %fusion.6.refs_16_), channel_id=1, source_target_pairs={{0,24},{8,0},{16,8},{24,16},{1,25},{9,1},{17,9},{25,17},{2,26},{10... | collective-permute-start | bytes 1179656 | tf_op jit(solution)/shard_map/ppermute | solution.py:72
  116.9 5.4 %collective-permute-done.18 = bf16[128,1536]{1,0:T(8,128)(2,1)S(1)} collective-permute-done((bf16[128,1536]{1,0:T(8,128)(2,1)}, bf16[128,1536]{1,0:T(8,128)(2,1)S(1)}, u32[]{:S(2)}, u32[]{:S(2)}) %collective-permute-start.18) | collective-permute-done | bytes 393248 | tf_op jit(solution)/shard_map/ppermute | solution.py:72
  126.8 3.7 %collective-permute-start.41 = (bf16[128,1536]{1,0:T(8,128)(2,1)S(1)}, bf16[128,1536]{1,0:T(8,128)(2,1)S(1)}, u32[]{:S(2)}, u32[]{:S(2)}) collective-permute-start(bf16[128,1536]{1,0:T(8,128)(2,1)S(1)} %collective-permute-done.39), channel_id=1, source_target_pairs={{0,24},{8,0},{16,8},{24,16},{1,25},{9,1},{17,9},{25,17},{2,26},{10... | collective-permute-start | bytes 1179656 | tf_op jit(solution)/shard_map/ppermute | solution.py:72
  131.7 3.2 %shard_map.78 = (bf16[256,768]{1,0:T(8,128)(2,1)S(1)}, bf16[256,768]{1,0:T(8,128)(2,1)S(1)}, bf16[256,768]{1,0:T(8,128)(2,1)S(1)}, bf16[256,768]{1,0:T(8,128)(2,1)S(1)}) custom-call(bf16[256,1536]{1,0:T(8,128)(2,1)S(1)} %bitcast.151, bf16[256,1536]{1,0:T(8,128)(2,1)S(1)} %bitcast.153, bf16[256,1536]{1,0:T(8,128)(2,1)S(1)} %bitcast.157, ...), custom_call_target="tpu_custom_call" | custom-call | flops 1024 | bytes 1024 | tf_op jit(solution)/shard_map/pallas_call | solution.py:50
  136.9 3.0 %collective-permute-start.43 = (bf16[128,1536]{1,0:T(8,128)(2,1)S(1)}, bf16[128,1536]{1,0:T(8,128)(2,1)S(1)}, u32[]{:S(2)}, u32[]{:S(2)}) collective-permute-start(bf16[128,1536]{1,0:T(8,128)(2,1)S(1)} %collective-permute-done.42), channel_id=1, source_target_pairs={{0,24},{8,0},{16,8},{24,16},{1,25},{9,1},{17,9},{25,17},{2,26},{10... | collective-permute-start | bytes 1179656 | tf_op jit(solution)/shard_map/ppermute | solution.py:72
  141.8 4.2 %shard_map.79.refs_21_ = bf16[1536,768]{1,0:T(8,128)(2,1)} custom-call(bf16[256,1536]{1,0:T(8,128)(2,1)S(1)} %bitcast.152, bf16[256,1536]{1,0:T(8,128)(2,1)S(1)} %bitcast.154, bf16[256,1536]{1,0:T(8,128)(2,1)S(1)} %bitcast.158, bf16[256,1536]{1,0:T(8,128)(2,1)S(1)} %bitcast.156, bf16[256,768]{1,0:T(8,128)(2,1)S(1)} %bitcast.183, ...), custom_call_target="tpu_custom_call" | custom-call | flops 2400000000 | bytes 1024 | tf_op jit(solution)/shard_map/pallas_call | solution.py:123
  146.0 2.9 %collective-permute-done.44.refs_20_ = bf16[128,1536]{1,0:T(8,128)(2,1)S(1)} collective-permute-done((bf16[128,1536]{1,0:T(8,128)(2,1)S(1)}, bf16[128,1536]{1,0:T(8,128)(2,1)S(1)}, u32[]{:S(2)}, u32[]{:S(2)}) %collective-permute-start.44) | collective-permute-done | bytes 393248 | tf_op jit(solution)/shard_map/ppermute | solution.py:72
  152.7 3.6 %collective-permute-done.36 = bf16[4,2,2,8,768]{4,3,2,1,0:T(8,128)(2,1)S(1)} collective-permute-done((bf16[4,2,2,8,768]{4,3,2,1,0:T(8,128)(2,1)S(1)}, bf16[4,2,2,8,768]{4,3,2,1,0:T(8,128)(2,1)S(1)}, u32[]{:S(2)}, u32[]{:S(2)}) %collective-permute-start.36) | collective-permute-done | bytes 196640 | tf_op jit(solution)/shard_map/ppermute | solution.py:72
  160.6 3.5 %collective-permute-done.52.refs_25_ = bf16[3,2,2,8,768]{4,3,2,1,0:T(8,128)(2,1)S(1)} collective-permute-done((bf16[3,2,2,8,768]{4,3,2,1,0:T(8,128)(2,1)S(1)}, bf16[3,2,2,8,768]{4,3,2,1,0:T(8,128)(2,1)S(1)}, u32[]{:S(2)}, u32[]{:S(2)}) %collective-permute-start.52) | collective-permute-done | bytes 147488 | tf_op jit(solution)/shard_map/ppermute | solution.py:72
  178.6 5.5 %shard_map.82 = bf16[768,1536]{1,0:T(8,128)(2,1)} custom-call(bf16[256,768]{1,0:T(8,128)(2,1)S(1)} %bitcast.149, bf16[256,768]{1,0:T(8,128)(2,1)S(1)} %bitcast.147, bf16[256,768]{1,0:T(8,128)(2,1)S(1)} %bitcast.173, bf16[256,768]{1,0:T(8,128)(2,1)S(1)} %bitcast.145, bf16[256,1536]{1,0:T(8,128)(2,1)S(1)} %bitcast.137, bf16[256,1536]{1,0:T(8,128)(2,1)} %bitcast.141, ...), custom_call_target="tpu_custom_call" | custom-call | flops 2400000000 | bytes 1024 | tf_op jit(solution)/shard_map/pallas_call | solution.py:123
  (251 shorter events, 67.0 us)
Async XLA Ops:
  3.5 12.0 %collective-permute-start = (bf16[3,2,1,8,768]{4,3,1,0,2:T(8,128)(2,1)S(1)}, bf16[3,2,1,8,768]{4,3,1,0,2:T(8,128)(2,1)S(1)}, u32[]{:S(2)}, u32[]{:S(2)}) collective-permute-start(bf16[3,2,1,8,768]{4,3,1,0,2:T(8,128)(2,1)S(1)} %maximum_bitcast_fusion), channel_id=1, source_target_pairs={{0,64},{64,0},{1,65},{65,1},{2,66},{66,2},{3,67},{67,3},{4,68},{68... | collective-permute-start | bytes 221192 | tf_op jit(solution)/shard_map/ppermute | solution.py:72
  5.0 14.7 %collective-permute-start.20 = (bf16[4,2,1,8,768]{4,3,2,1,0:T(8,128)(2,1)S(1)}, bf16[4,2,1,8,768]{4,3,2,1,0:T(8,128)(2,1)S(1)}, u32[]{:S(2)}, u32[]{:S(2)}) collective-permute-start(bf16[4,2,1,8,768]{4,3,2,1,0:T(8,128)(2,1)S(1)} %fusion.26), channel_id=1, source_target_pairs={{0,64},{64,0},{1,65},{65,1},{2,66},{66,2},{3,67},{67,3},{4,68},{68... | collective-permute-start | bytes 294920 | tf_op jit(solution)/shard_map/ppermute | solution.py:72
  15.8 11.7 %collective-permute-start.6 = (bf16[3,2,2,8,768]{4,3,1,0,2:T(8,128)(2,1)S(1)}, bf16[3,2,2,8,768]{4,3,1,0,2:T(8,128)(2,1)S(1)}, u32[]{:S(2)}, u32[]{:S(2)}) collective-permute-start(bf16[3,2,2,8,768]{4,3,1,0,2:T(8,128)(2,1)S(1)} %pad_maximum_fusion.16), channel_id=1, source_target_pairs={{0,2},{1,3},{2,0},{3,1},{4,6},{5,7},{6,4},{7,5},{8,10},{9,11},{10,... | collective-permute-start | bytes 442376 | tf_op jit(solution)/shard_map/ppermute | solution.py:72
  21.2 10.4 %collective-permute-start.23 = (bf16[4,2,2,8,768]{4,3,2,1,0:T(8,128)(2,1)S(1)}, bf16[4,2,2,8,768]{4,3,2,1,0:T(8,128)(2,1)S(1)}, u32[]{:S(2)}, u32[]{:S(2)}) collective-permute-start(bf16[4,2,2,8,768]{4,3,2,1,0:T(8,128)(2,1)S(1)} %pad_maximum_fusion.15), channel_id=1, source_target_pairs={{0,1},{1,2},{2,3},{3,0},{4,5},{5,6},{6,7},{7,4},{8,9},{9,10},{10,1... | collective-permute-start | bytes 589832 | tf_op jit(solution)/shard_map/ppermute | solution.py:72
  23.2 12.4 %collective-permute-start.22 = (bf16[4,2,2,8,768]{4,3,2,1,0:T(8,128)(2,1)S(1)}, bf16[4,2,2,8,768]{4,3,2,1,0:T(8,128)(2,1)S(1)}, u32[]{:S(2)}, u32[]{:S(2)}) collective-permute-start(bf16[4,2,2,8,768]{4,3,2,1,0:T(8,128)(2,1)S(1)} %pad_maximum_fusion.15), channel_id=1, source_target_pairs={{0,2},{1,3},{2,0},{3,1},{4,6},{5,7},{6,4},{7,5},{8,10},{9,11},{10,... | collective-permute-start | bytes 589832 | tf_op jit(solution)/shard_map/ppermute | solution.py:72
  23.5 12.1 %collective-permute-start.21 = (bf16[4,2,2,8,768]{4,3,2,1,0:T(8,128)(2,1)S(1)}, bf16[4,2,2,8,768]{4,3,2,1,0:T(8,128)(2,1)S(1)}, u32[]{:S(2)}, u32[]{:S(2)}) collective-permute-start(bf16[4,2,2,8,768]{4,3,2,1,0:T(8,128)(2,1)S(1)} %pad_maximum_fusion.15), channel_id=1, source_target_pairs={{0,3},{1,0},{2,1},{3,2},{4,7},{5,4},{6,5},{7,6},{8,11},{9,8},{10,9... | collective-permute-start | bytes 589832 | tf_op jit(solution)/shard_map/ppermute | solution.py:72
  27.8 13.8 %collective-permute-start.10 = (bf16[128,1536]{1,0:T(8,128)(2,1)S(1)}, bf16[128,1536]{1,0:T(8,128)(2,1)S(1)}, u32[]{:S(2)}, u32[]{:S(2)}) collective-permute-start(bf16[128,1536]{1,0:T(8,128)(2,1)S(1)} %get-tuple-element.197), channel_id=1, source_target_pairs={{0,8},{8,16},{16,24},{24,0},{1,9},{9,17},{17,25},{25,1},{2,10},{10... | collective-permute-start | bytes 1179656 | tf_op jit(solution)/shard_map/ppermute | solution.py:72
  31.6 12.5 %collective-permute-start.12 = (bf16[128,1536]{1,0:T(8,128)(2,1)S(1)}, bf16[128,1536]{1,0:T(8,128)(2,1)S(1)}, u32[]{:S(2)}, u32[]{:S(2)}) collective-permute-start(bf16[128,1536]{1,0:T(8,128)(2,1)S(1)} %get-tuple-element.198), channel_id=1, source_target_pairs={{0,24},{8,0},{16,8},{24,16},{1,25},{9,1},{17,9},{25,17},{2,26},{10... | collective-permute-start | bytes 1179656 | tf_op jit(solution)/shard_map/ppermute | solution.py:72
  35.8 12.2 %collective-permute-start.24 = (bf16[4,2,8,8,768]{4,3,2,1,0:T(8,128)(2,1)S(1)}, bf16[4,2,8,8,768]{4,3,2,1,0:T(8,128)(2,1)S(1)}, u32[]{:S(2)}, u32[]{:S(2)}) collective-permute-start(bf16[4,2,8,8,768]{4,3,2,1,0:T(8,128)(2,1)S(1)} %pad_maximum_fusion.4), channel_id=1, source_target_pairs={{0,32},{32,0},{1,33},{33,1},{2,34},{34,2},{3,35},{35,3},{4,36},{36... | collective-permute-start | bytes 2359304 | tf_op jit(solution)/shard_map/ppermute | solution.py:72
  41.7 21.7 %collective-permute-start.11 = (bf16[2,128,1536]{2,1,0:T(8,128)(2,1)S(1)}, bf16[2,128,1536]{2,1,0:T(8,128)(2,1)S(1)}, u32[]{:S(2)}, u32[]{:S(2)}) collective-permute-start(bf16[2,128,1536]{2,1,0:T(8,128)(2,1)S(1)} %fusion.12), channel_id=1, source_target_pairs={{0,8},{8,16},{16,24},{24,0},{1,9},{9,17},{17,25},{25,1},{2,10},{10... | collective-permute-start | bytes 2359304 | tf_op jit(solution)/shard_map/ppermute | solution.py:72
  44.2 21.8 %collective-permute-start.13 = (bf16[2,128,1536]{2,1,0:T(8,128)(2,1)S(1)}, bf16[2,128,1536]{2,1,0:T(8,128)(2,1)S(1)}, u32[]{:S(2)}, u32[]{:S(2)}) collective-permute-start(bf16[2,128,1536]{2,1,0:T(8,128)(2,1)S(1)} %fusion.14), channel_id=1, source_target_pairs={{0,24},{8,0},{16,8},{24,16},{1,25},{9,1},{17,9},{25,17},{2,26},{10... | collective-permute-start | bytes 2359304 | tf_op jit(solution)/shard_map/ppermute | solution.py:72
  53.6 18.8 %collective-permute-start.26 = (bf16[128,1536]{1,0:T(8,128)(2,1)S(1)}, bf16[128,1536]{1,0:T(8,128)(2,1)S(1)}, u32[]{:S(2)}, u32[]{:S(2)}) collective-permute-start(bf16[128,1536]{1,0:T(8,128)(2,1)S(1)} %get-tuple-element.195), channel_id=1, source_target_pairs={{0,24},{8,0},{16,8},{24,16},{1,25},{9,1},{17,9},{25,17},{2,26},{10... | collective-permute-start | bytes 1179656 | tf_op jit(solution)/shard_map/ppermute | solution.py:72
  53.7 18.7 %collective-permute-start.25 = (bf16[128,1536]{1,0:T(8,128)(2,1)S(1)}, bf16[128,1536]{1,0:T(8,128)(2,1)S(1)}, u32[]{:S(2)}, u32[]{:S(2)}) collective-permute-start(bf16[128,1536]{1,0:T(8,128)(2,1)S(1)} %get-tuple-element.196), channel_id=1, source_target_pairs={{0,8},{8,16},{16,24},{24,0},{1,9},{9,17},{17,25},{25,1},{2,10},{10... | collective-permute-start | bytes 1179656 | tf_op jit(solution)/shard_map/ppermute | solution.py:72
  66.1 10.5 %collective-permute-start.14 = (bf16[128,1536]{1,0:T(8,128)(2,1)S(1)}, bf16[128,1536]{1,0:T(8,128)(2,1)S(1)}, u32[]{:S(2)}, u32[]{:S(2)}) collective-permute-start(bf16[128,1536]{1,0:T(8,128)(2,1)S(1)} %fusion.9.refs_14_), channel_id=1, source_target_pairs={{0,4},{4,0},{1,5},{5,1},{2,6},{6,2},{3,7},{7,3},{8,12},{12,8},{9,1... | collective-permute-start | bytes 1179656 | tf_op jit(solution)/shard_map/ppermute | solution.py:72
  72.5 22.2 %collective-permute-start.27 = (bf16[2,128,1536]{2,1,0:T(8,128)(2,1)S(1)}, bf16[2,128,1536]{2,1,0:T(8,128)(2,1)S(1)}, u32[]{:S(2)}, u32[]{:S(2)}) collective-permute-start(bf16[2,128,1536]{2,1,0:T(8,128)(2,1)S(1)} %fusion.16), channel_id=1, source_target_pairs={{0,8},{8,16},{16,24},{24,0},{1,9},{9,17},{17,25},{25,1},{2,10},{10... | collective-permute-start | bytes 2359304 | tf_op jit(solution)/shard_map/ppermute | solution.py:72
  72.7 22.0 %collective-permute-start.28 = (bf16[2,128,1536]{2,1,0:T(8,128)(2,1)S(1)}, bf16[2,128,1536]{2,1,0:T(8,128)(2,1)S(1)}, u32[]{:S(2)}, u32[]{:S(2)}) collective-permute-start(bf16[2,128,1536]{2,1,0:T(8,128)(2,1)S(1)} %fusion.18), channel_id=1, source_target_pairs={{0,24},{8,0},{16,8},{24,16},{1,25},{9,1},{17,9},{25,17},{2,26},{10... | collective-permute-start | bytes 2359304 | tf_op jit(solution)/shard_map/ppermute | solution.py:72
  77.9 10.7 %collective-permute-start.15 = (bf16[128,1536]{1,0:T(8,128)(2,1)}, bf16[128,1536]{1,0:T(8,128)(2,1)}, u32[]{:S(2)}, u32[]{:S(2)}) collective-permute-start(bf16[128,1536]{1,0:T(8,128)(2,1)} %multiply_convert_fusion), channel_id=1, source_target_pairs={{0,4},{4,0},{1,5},{5,1},{2,6},{6,2},{3,7},{7,3},{8,12},{12,8},{9,1... | collective-permute-start | bytes 1179656 | tf_op jit(solution)/shard_map/ppermute | solution.py:72
  80.6 20.1 %collective-permute-start.17 = (bf16[128,1536]{1,0:T(8,128)(2,1)}, bf16[128,1536]{1,0:T(8,128)(2,1)}, u32[]{:S(2)}, u32[]{:S(2)}) collective-permute-start(bf16[128,1536]{1,0:T(8,128)(2,1)} %multiply_convert_fusion), channel_id=1, source_target_pairs={{0,8},{8,16},{16,24},{24,0},{1,9},{9,17},{17,25},{25,1},{2,10},{10... | collective-permute-start | bytes 1179656 | tf_op jit(solution)/shard_map/ppermute | solution.py:72
  80.6 20.1 %collective-permute-start.16 = (bf16[128,1536]{1,0:T(8,128)(2,1)}, bf16[128,1536]{1,0:T(8,128)(2,1)}, u32[]{:S(2)}, u32[]{:S(2)}) collective-permute-start(bf16[128,1536]{1,0:T(8,128)(2,1)} %multiply_convert_fusion), channel_id=1, source_target_pairs={{0,24},{8,0},{16,8},{24,16},{1,25},{9,1},{17,9},{25,17},{2,26},{10... | collective-permute-start | bytes 1179656 | tf_op jit(solution)/shard_map/ppermute | solution.py:72
  96.0 12.4 %collective-permute-start.29 = (bf16[128,1536]{1,0:T(8,128)(2,1)}, bf16[128,1536]{1,0:T(8,128)(2,1)}, u32[]{:S(2)}, u32[]{:S(2)}) collective-permute-start(bf16[128,1536]{1,0:T(8,128)(2,1)} %fusion.7), channel_id=1, source_target_pairs={{0,4},{4,0},{1,5},{5,1},{2,6},{6,2},{3,7},{7,3},{8,12},{12,8},{9,1... | collective-permute-start | bytes 1179656 | tf_op jit(solution)/shard_map/ppermute | solution.py:72
  100.7 29.8 %collective-permute-start.30 = (bf16[128,1536]{1,0:T(8,128)(2,1)}, bf16[128,1536]{1,0:T(8,128)(2,1)S(1)}, u32[]{:S(2)}, u32[]{:S(2)}) collective-permute-start(bf16[128,1536]{1,0:T(8,128)(2,1)} %collective-permute-done.16), channel_id=1, source_target_pairs={{0,24},{8,0},{16,8},{24,16},{1,25},{9,1},{17,9},{25,17},{2,26},{10... | collective-permute-start | bytes 1179656 | tf_op jit(solution)/shard_map/ppermute | solution.py:72
  104.0 18.3 %collective-permute-start.18 = (bf16[128,1536]{1,0:T(8,128)(2,1)}, bf16[128,1536]{1,0:T(8,128)(2,1)S(1)}, u32[]{:S(2)}, u32[]{:S(2)}) collective-permute-start(bf16[128,1536]{1,0:T(8,128)(2,1)} %collective-permute-done.15.refs_15_), channel_id=1, source_target_pairs={{0,24},{8,0},{16,8},{24,16},{1,25},{9,1},{17,9},{25,17},{2,26},{10... | collective-permute-start | bytes 1179656 | tf_op jit(solution)/shard_map/ppermute | solution.py:72
  110.9 24.9 %collective-permute-start.42 = (bf16[128,1536]{1,0:T(8,128)(2,1)S(1)}, bf16[128,1536]{1,0:T(8,128)(2,1)S(1)}, u32[]{:S(2)}, u32[]{:S(2)}) collective-permute-start(bf16[128,1536]{1,0:T(8,128)(2,1)S(1)} %fusion.6.refs_16_), channel_id=1, source_target_pairs={{0,4},{4,0},{1,5},{5,1},{2,6},{6,2},{3,7},{7,3},{8,12},{12,8},{9,1... | collective-permute-start | bytes 1179656 | tf_op jit(solution)/shard_map/ppermute | solution.py:72
  113.7 12.5 %collective-permute-start.40 = (bf16[128,1536]{1,0:T(8,128)(2,1)S(1)}, bf16[128,1536]{1,0:T(8,128)(2,1)S(1)}, u32[]{:S(2)}, u32[]{:S(2)}) collective-permute-start(bf16[128,1536]{1,0:T(8,128)(2,1)S(1)} %fusion.6.refs_16_), channel_id=1, source_target_pairs={{0,8},{8,16},{16,24},{24,0},{1,9},{9,17},{17,25},{25,1},{2,10},{10... | collective-permute-start | bytes 1179656 | tf_op jit(solution)/shard_map/ppermute | solution.py:72
  113.7 13.1 %collective-permute-start.39 = (bf16[128,1536]{1,0:T(8,128)(2,1)S(1)}, bf16[128,1536]{1,0:T(8,128)(2,1)S(1)}, u32[]{:S(2)}, u32[]{:S(2)}) collective-permute-start(bf16[128,1536]{1,0:T(8,128)(2,1)S(1)} %fusion.6.refs_16_), channel_id=1, source_target_pairs={{0,24},{8,0},{16,8},{24,16},{1,25},{9,1},{17,9},{25,17},{2,26},{10... | collective-permute-start | bytes 1179656 | tf_op jit(solution)/shard_map/ppermute | solution.py:72
  126.8 25.2 %collective-permute-start.41 = (bf16[128,1536]{1,0:T(8,128)(2,1)S(1)}, bf16[128,1536]{1,0:T(8,128)(2,1)S(1)}, u32[]{:S(2)}, u32[]{:S(2)}) collective-permute-start(bf16[128,1536]{1,0:T(8,128)(2,1)S(1)} %collective-permute-done.39), channel_id=1, source_target_pairs={{0,24},{8,0},{16,8},{24,16},{1,25},{9,1},{17,9},{25,17},{2,26},{10... | collective-permute-start | bytes 1179656 | tf_op jit(solution)/shard_map/ppermute | solution.py:72
  136.6 12.4 %collective-permute-start.44 = (bf16[128,1536]{1,0:T(8,128)(2,1)S(1)}, bf16[128,1536]{1,0:T(8,128)(2,1)S(1)}, u32[]{:S(2)}, u32[]{:S(2)}) collective-permute-start(bf16[128,1536]{1,0:T(8,128)(2,1)S(1)} %collective-permute-done.42), channel_id=1, source_target_pairs={{0,8},{8,16},{16,24},{24,0},{1,9},{9,17},{17,25},{25,1},{2,10},{10... | collective-permute-start | bytes 1179656 | tf_op jit(solution)/shard_map/ppermute | solution.py:72
  136.9 12.1 %collective-permute-start.43 = (bf16[128,1536]{1,0:T(8,128)(2,1)S(1)}, bf16[128,1536]{1,0:T(8,128)(2,1)S(1)}, u32[]{:S(2)}, u32[]{:S(2)}) collective-permute-start(bf16[128,1536]{1,0:T(8,128)(2,1)S(1)} %collective-permute-done.42), channel_id=1, source_target_pairs={{0,24},{8,0},{16,8},{24,16},{1,25},{9,1},{17,9},{25,17},{2,26},{10... | collective-permute-start | bytes 1179656 | tf_op jit(solution)/shard_map/ppermute | solution.py:72
  140.3 11.8 %collective-permute-start.38 = (bf16[4,2,2,8,768]{4,3,2,1,0:T(8,128)(2,1)S(1)}, bf16[4,2,2,8,768]{4,3,2,1,0:T(8,128)(2,1)S(1)}, u32[]{:S(2)}, u32[]{:S(2)}) collective-permute-start(bf16[4,2,2,8,768]{4,3,2,1,0:T(8,128)(2,1)S(1)} %get-tuple-element.191), channel_id=1, source_target_pairs={{0,3},{1,0},{2,1},{3,2},{4,7},{5,4},{6,5},{7,6},{8,11},{9,8},{10,9... | collective-permute-start | bytes 589832 | tf_op jit(solution)/shard_map/ppermute | solution.py:72
  141.4 11.2 %collective-permute-start.37 = (bf16[4,2,2,8,768]{4,3,2,1,0:T(8,128)(2,1)S(1)}, bf16[4,2,2,8,768]{4,3,2,1,0:T(8,128)(2,1)S(1)}, u32[]{:S(2)}, u32[]{:S(2)}) collective-permute-start(bf16[4,2,2,8,768]{4,3,2,1,0:T(8,128)(2,1)S(1)} %get-tuple-element.192), channel_id=1, source_target_pairs={{0,2},{1,3},{2,0},{3,1},{4,6},{5,7},{6,4},{7,5},{8,10},{9,11},{10,... | collective-permute-start | bytes 589832 | tf_op jit(solution)/shard_map/ppermute | solution.py:72
  149.0 11.5 %collective-permute-start.49 = (bf16[128,1536]{1,0:T(8,128)(2,1)S(1)}, bf16[128,1536]{1,0:T(8,128)(2,1)S(1)}, u32[]{:S(2)}, u32[]{:S(2)}) collective-permute-start(bf16[128,1536]{1,0:T(8,128)(2,1)S(1)} %collective-permute-done.44.refs_20_), channel_id=1, source_target_pairs={{0,8},{8,16},{16,24},{24,0},{1,9},{9,17},{17,25},{25,1},{2,10},{10... | collective-permute-start | bytes 1179656 | tf_op jit(solution)/shard_map/ppermute | solution.py:72
  156.4 12.5 %collective-permute-start.45 = (bf16[4,2,8,768]{3,2,1,0:T(8,128)(2,1)S(1)}, bf16[4,2,8,768]{3,2,1,0:T(8,128)(2,1)S(1)}, u32[]{:S(2)}, u32[]{:S(2)}) collective-permute-start(bf16[4,2,8,768]{3,2,1,0:T(8,128)(2,1)S(1)} %slice_bitcast_fusion.6), channel_id=1, source_target_pairs={{0,64},{64,0},{1,65},{65,1},{2,66},{66,2},{3,67},{67,3},{4,68},{68... | collective-permute-start | bytes 294920 | tf_op jit(solution)/shard_map/ppermute | solution.py:72
  (63 other events, 454.9 us)
